TPU v7x, 32 devices: a whole 2x2x4 slice. The times are simulated.
32 devices in a mesh: section: 4 (over x, core), tensor: 8 (over z, y).
Axes of the slice: x: 2, y: 2, z: 4, core: 2. Of those that a mesh axis runs over, the one named last changes fastest.
Arguments:
- hidden: bfloat16 [4, 256, 8192], P('section', 'tensor'), may hold values from -60 to 60
- norm_gain: float32 [8192], replicated, may hold values from 0.1 to 1.9
- lengths: int32 [4], P('section'), may hold values from 64 to 256
- query_param: float32 [8192, 4096], P(('section', 'tensor')), may hold values from -1.3258252 to 1.3258252
- query_grad: float32 [8192, 4096], P(('section', 'tensor')), may hold values from -0.006 to 0.006
- query_moment: float32 [8192, 4096], P(('section', 'tensor')), may hold values from -0.006 to 0.006
- query_second: float32 [8192, 4096], P(('section', 'tensor')), may hold values from 1e-07 to 1e-05
- keyval_param: float32 [8192, 1024], P(('section', 'tensor')), may hold values from -0.06629126 to 0.06629126
- keyval_gradient: float32 [8192, 1024], P(('section', 'tensor')), may hold values from -0.006 to 0.006
- keyval_first_moment: float32 [8192, 1024], P(('section', 'tensor')), may hold values from -0.006 to 0.006
- keyval_second_moment: float32 [8192, 1024], P(('section', 'tensor')), may hold values from 1e-07 to 1e-05
- output_param: float32 [8192, 4096], P(('section', 'tensor')), may hold values from -0.25 to 0.25
- output_grad: float32 [8192, 4096], P(('section', 'tensor')), may hold values from -0.006 to 0.006
- output_moment: float32 [8192, 4096], P(('section', 'tensor')), may hold values from -0.006 to 0.006
- output_second: float32 [8192, 4096], P(('section', 'tensor')), may hold values from 1e-07 to 1e-05
Outputs:
- mixed: bfloat16 [4, 256, 8192], P('section', 'tensor')
All inputs are finite; a program needn't handle non-finite values.
Results may differ from a plain program's by a relative error of at most 0.017.
Values may be sent and summed in bfloat16 or wider, within the bound.
A program may use at most 128 MiB of HBM per device.

v0:
```python
import math

import jax
import jax.numpy as jnp
from jax import lax
from jax.sharding import PartitionSpec as P

QUERY_HEADS_LOCAL = 32
KEYVAL_HEADS = 4
HEAD_DIMENSION = 128


learn_rate = 0.015
beta_one = 0.5
beta_two = 0.9
adam_step = 1000.0
adam_eps = 1e-08
decay_rate = 0.1
norm_eps = 1e-06
rope_base = 1000000.0
masked_score = -1e30


def adam_update(current, gradient, moment, second):
    moment_new = beta_one * moment + (1.0 - beta_one) * gradient
    second_new = beta_two * second + (1.0 - beta_two) * gradient * gradient
    corrected = moment_new / (1.0 - beta_one**adam_step)
    denominator = jnp.sqrt(second_new / (1.0 - beta_two**adam_step)) + adam_eps
    return (current - learn_rate * (corrected / denominator + decay_rate * current)).astype(
        jnp.bfloat16
    )


def normalize(hidden, norm_gain):
    values = hidden.astype(jnp.float32)
    factor = lax.rsqrt(jnp.mean(values * values, axis=-1, keepdims=True) + norm_eps)
    return (values * factor * norm_gain).astype(jnp.bfloat16)


def rotary_embed(values, token_positions):
    half_width = values.shape[-1] // 2
    frequency = rope_base ** (-jnp.arange(half_width, dtype=jnp.float32) * 2.0 / values.shape[-1])
    angles = token_positions.astype(jnp.float32)[:, None] * frequency[None, :]
    cosine_table = jnp.concatenate([jnp.cos(angles), jnp.cos(angles)], axis=-1)
    sine_table = jnp.concatenate([jnp.sin(angles), jnp.sin(angles)], axis=-1)
    first_half = values[..., :half_width]
    second_half = values[..., half_width:]
    rotated = jnp.concatenate([-second_half, first_half], axis=-1)
    return values * cosine_table + rotated * sine_table


def on_device(
    hidden,
    norm_gain,
    lengths,
    query_param,
    query_grad,
    query_moment,
    query_second,
    keyval_param,
    keyval_gradient,
    keyval_first_moment,
    keyval_second_moment,
    output_param,
    output_grad,
    output_moment,
    output_second,
):
    tensor_count = lax.axis_size("tensor")
    section_size = lax.axis_size("section")
    query_weight = adam_update(query_param, query_grad, query_moment, query_second)
    keyval_matrix = adam_update(
        keyval_param, keyval_gradient, keyval_first_moment, keyval_second_moment
    )
    output_weight = adam_update(output_param, output_grad, output_moment, output_second)
    local_rows = normalize(hidden[0], norm_gain)
    normed = lax.all_gather(local_rows, "tensor", axis=0, tiled=True)
    sequence = normed.shape[0]
    model_width = normed.shape[1]
    weight_row_block = query_weight.shape[0]
    heads_here = QUERY_HEADS_LOCAL // tensor_count
    head_columns = heads_here * HEAD_DIMENSION
    head_copies = tensor_count // KEYVAL_HEADS
    spread_heads = keyval_matrix.reshape(weight_row_block, 2, KEYVAL_HEADS, HEAD_DIMENSION)
    spread_heads = (
        jnp.repeat(spread_heads, head_copies, axis=2)
        .transpose(0, 2, 1, 3)
        .reshape(weight_row_block, tensor_count * 2 * HEAD_DIMENSION)
    )
    query_start = jnp.zeros((sequence, head_columns), jnp.float32)
    query_slice, keyval_slice = (
        lax.all_to_all(query_weight, "tensor", split_axis=1, concat_axis=0, tiled=True),
        lax.all_to_all(spread_heads, "tensor", split_axis=1, concat_axis=0, tiled=True),
    )
    query_total = query_start
    query_rows = lax.all_gather(query_slice, "section", axis=0, tiled=True)
    keyval_rows = lax.all_gather(keyval_slice, "section", axis=0, tiled=True)
    columns = lax.slice_in_dim(normed, 0, query_rows.shape[0], axis=1)
    query_total = query_total + jnp.dot(columns, query_rows, preferred_element_type=jnp.float32)
    keyval_total = jnp.dot(columns, keyval_rows, preferred_element_type=jnp.float32)
    key_block = keyval_total[:, :HEAD_DIMENSION]
    value_block = keyval_total[:, HEAD_DIMENSION:]
    token_positions = jnp.arange(sequence)
    query_heads = rotary_embed(
        query_total.reshape(sequence, heads_here, HEAD_DIMENSION).transpose(1, 0, 2),
        token_positions,
    ).astype(jnp.bfloat16)
    key_head_rows = rotary_embed(key_block, token_positions).astype(jnp.bfloat16)
    value_head_rows = value_block.astype(jnp.bfloat16)
    scores = jnp.einsum(
        "hqd,kd->hqk", query_heads, key_head_rows, preferred_element_type=jnp.float32
    ) / math.sqrt(HEAD_DIMENSION)
    allowed = (token_positions[None, :] <= token_positions[:, None]) & (
        token_positions[None, :] < lengths[0]
    )
    scores = jnp.where(allowed[None], scores, masked_score)
    row_max = jnp.max(scores, axis=-1, keepdims=True)
    exponent = jnp.exp(scores - row_max)
    attention = (exponent / jnp.sum(exponent, axis=-1, keepdims=True)).astype(jnp.bfloat16)
    head_out = jnp.einsum(
        "hqk,kd->hqd", attention, value_head_rows, preferred_element_type=jnp.float32
    ).astype(jnp.bfloat16)
    head_out = head_out.transpose(1, 0, 2).reshape(sequence, head_columns)
    out_rows = lax.all_gather(output_weight, "section", axis=0, tiled=True)
    feature_count = out_rows.shape[0]
    piece = lax.all_gather(head_out, "tensor", axis=1, tiled=True)
    groups = piece.shape[1] // head_columns
    heads_part = piece.reshape(sequence, groups, head_columns)
    weights_part = lax.slice_in_dim(out_rows, 0, piece.shape[1], axis=1).reshape(
        feature_count, groups, head_columns
    )
    partial_terms = jnp.einsum(
        "sgc,fgc->gsf", heads_part, weights_part, preferred_element_type=jnp.float32
    )
    summed = jnp.zeros((sequence, feature_count), jnp.float32) + jnp.sum(
        partial_terms.astype(jnp.bfloat16).astype(jnp.float32), axis=0
    )
    feature_part = summed.astype(jnp.bfloat16)
    arrived = lax.all_to_all(feature_part, "tensor", split_axis=0, concat_axis=1, tiled=True)
    token_rows = arrived.shape[0]
    ordered = (
        arrived.reshape(token_rows, tensor_count, section_size, weight_row_block)
        .transpose(0, 2, 1, 3)
        .reshape(token_rows, model_width)
    )
    return ordered[None]


def solution(mesh):
    return jax.shard_map(
        on_device,
        mesh=mesh,
        in_specs=(
            P("section", "tensor", None),
            P(),
            P("section"),
            P(("section", "tensor"), None),
            P(("section", "tensor"), None),
            P(("section", "tensor"), None),
            P(("section", "tensor"), None),
            P(("section", "tensor"), None),
            P(("section", "tensor"), None),
            P(("section", "tensor"), None),
            P(("section", "tensor"), None),
            P(("section", "tensor"), None),
            P(("section", "tensor"), None),
            P(("section", "tensor"), None),
            P(("section", "tensor"), None),
        ),
        out_specs=P("section", "tensor", None),
        check_vma=False,
    )
```

profile of v0, /device:TPU:0, one launch (start us, length us, event | category | flops | bytes accessed | tf_op | source)
XLA Modules:
  0.0 353.7 jit_solution(2134100142875917133)
XLA Ops:
  6.5 0.0 all-gather.6.cloned.1.call-start
  6.5 1.2 fusion.20
  7.8 2.0 fusion.22
  9.8 0.0 all-gather.6.cloned.1.call-update
  9.9 0.0 all-gather.10.cloned.1.call-start
  9.9 2.9 fusion.30
  12.8 0.4 reshape.91
  13.2 0.4 copy.54
  13.6 0.5 broadcast_in_dim.11
  14.1 0.7 all_to_all.44
  14.8 49.4 %all_to_all.54 = bf16[256,8,256]{2,0,1:T(8,128)(2,1)} all-to-all(bf16[256,8,256]{2,0,1:T(8,128)(2,1)S(1)} %all_to_all.44), channel_id=1, replica_groups=mesh['section'=4,'tensor'=8] {'tensor'}, dimensions={1} | all-to-all | bytes 2097152 | tf_op jit(solution)/shard_map/all_to_all | solution.py:93
  64.3 0.0 all-gather.10.cloned.1.call-update
  64.3 0.0 all-gather.8.cloned.1.call-start
  64.3 5.7 %copy.49 = f32[256,4096]{0,1:T(8,128)} copy(f32[256,4096]{1,0:T(8,128)} %param.18) | data formatting | bytes 8388608 | tf_op args[3]
  70.0 5.6 %copy.44 = f32[256,4096]{0,1:T(8,128)} copy(f32[256,4096]{1,0:T(8,128)} %param.19) | data formatting | bytes 8388608 | tf_op args[4]
  75.6 5.6 %copy.45 = f32[256,4096]{0,1:T(8,128)} copy(f32[256,4096]{1,0:T(8,128)} %param.21) | data formatting | bytes 8388608 | tf_op args[6]
  81.2 5.6 %copy.43 = f32[256,4096]{0,1:T(8,128)} copy(f32[256,4096]{1,0:T(8,128)} %param.20) | data formatting | bytes 8388608 | tf_op args[5]
  86.8 7.4 %fusion.16 = bf16[256,4096]{0,1:T(8,128)(2,1)S(1)} fusion(f32[256,4096]{0,1:T(8,128)} %copy.49, f32[256,4096]{0,1:T(8,128)} %copy.44, f32[256,4096]{0,1:T(8,128)} %copy.45, f32[256,4096]{0,1:T(8,128)} %copy.43), kind=kLoop, calls=%fused_computation.19 | loop fusion | flops 13631488 | bytes 18874368 | tf_op jit(solution)/shard_map/convert_element_type | solution.py:29
  94.3 55.8 %all_to_all.55 = bf16[256,8,512]{0,2,1:T(8,128)(2,1)S(1)} all-to-all(bf16[256,8,512]{0,2,1:T(8,128)(2,1)S(1)} %bitcast.73), channel_id=1, replica_groups=mesh['section'=4,'tensor'=8] {'tensor'}, dimensions={1} | all-to-all | bytes 4194304 | tf_op jit(solution)/shard_map/all_to_all | solution.py:92
  150.1 2.4 copy.50
  152.5 0.0 all-gather.8.cloned.1.call-update
  152.5 0.0 all-gather.14.cloned.1.call-start
  152.6 5.6 %copy.63 = f32[256,4096]{0,1:T(8,128)} copy(f32[256,4096]{1,0:T(8,128)} %param.26) | data formatting | bytes 8388608 | tf_op args[11]
  158.2 6.0 %copy.58 = f32[256,4096]{0,1:T(8,128)} copy(f32[256,4096]{1,0:T(8,128)} %param.27) | data formatting | bytes 8388608 | tf_op args[12]
  164.2 5.6 %copy.59 = f32[256,4096]{0,1:T(8,128)} copy(f32[256,4096]{1,0:T(8,128)} %param.29) | data formatting | bytes 8388608 | tf_op args[14]
  169.8 5.6 %copy.57 = f32[256,4096]{0,1:T(8,128)} copy(f32[256,4096]{1,0:T(8,128)} %param.28) | data formatting | bytes 8388608 | tf_op args[13]
  175.4 8.3 %fusion.15 = bf16[256,4096]{0,1:T(8,128)(2,1)} fusion(f32[256,4096]{0,1:T(8,128)} %copy.63, f32[256,4096]{0,1:T(8,128)} %copy.58, f32[256,4096]{0,1:T(8,128)} %copy.59, f32[256,4096]{0,1:T(8,128)} %copy.57), kind=kLoop, calls=%fused_computation.18 | loop fusion | flops 13631488 | bytes 18874368 | tf_op jit(solution)/shard_map/convert_element_type | solution.py:29
  183.7 0.0 all-gather.14.cloned.1.call-update
  183.7 0.2 all-gather.12.cloned.1.call-start
  184.6 0.3 multiply_cosine_fusion
  185.0 0.1 copy.53
  185.1 0.1 copy.52
  185.2 0.1 fusion.36
  185.3 0.0 all-gather.6.cloned.1.call-done
  185.3 0.0 all-gather.10.cloned.1.call-done
  185.3 5.3 %fusion.58 = f32[256,256]{0,1:T(8,128)S(1)} fusion(bf16[256,8192]{1,0:T(8,128)(2,1)} %all-gather.6.cloned.1.call-done, bf16[8192,256]{1,0:T(8,128)(2,1)} %all-gather.10.cloned.1.call-done), kind=kOutput, calls=%fused_computation.72 | convolution fusion | flops 1073741824 | bytes 8650752 | tf_op jit(solution)/shard_map/dot_general | solution.py:100
  190.7 18.7 %all-gather.8.cloned.1.call-done = bf16[8192,512]{1,0:T(8,128)(2,1)} async-done(((bf16[2048,512]{1,0:T(8,128)(2,1)}), bf16[8192,512]{1,0:T(8,128)(2,1)}) %all-gather.8.cloned.1.call-update) | async-done | bytes 8388624 | tf_op jit(solution)/shard_map/all_gather | solution.py:96
  209.4 7.0 %convolution_bitcast_fusion = f32[32,4,8,128]{3,2,1,0:T(8,128)S(1)} fusion(bf16[256,8192]{1,0:T(8,128)(2,1)} %all-gather.6.cloned.1.call-done, bf16[8192,512]{1,0:T(8,128)(2,1)} %all-gather.8.cloned.1.call-done), kind=kOutput, calls=%fused_computation.27 | convolution fusion | flops 2147483648 | bytes 13107200 | tf_op jit(solution)/shard_map/dot_general | solution.py:99
  216.4 0.2 slice_negate_fusion
  216.6 0.7 fusion.53
  217.3 0.5 fusion.19
  217.8 1.1 convolution_convert_fusion
  218.9 0.0 all-gather.12.cloned.1.call-update
  218.9 51.3 %all-gather.14.cloned.1.call-done = bf16[1024,4096]{0,1:T(8,128)(2,1)} async-done(((bf16[256,4096]{0,1:T(8,128)(2,1)}), bf16[1024,4096]{0,1:T(8,128)(2,1)}) %all-gather.14.cloned.1.call-update) | async-done | bytes 8388624 | tf_op jit(solution)/shard_map/all_gather | solution.py:124
  270.2 51.3 %all-gather.12.cloned.1.call-done = bf16[256,4096]{0,1:T(8,128)(2,1)} async-done(((bf16[256,512]{0,1:T(8,128)(2,1)}), bf16[256,4096]{0,1:T(8,128)(2,1)}) %all-gather.12.cloned.1.call-update) | async-done | bytes 2097168 | tf_op jit(solution)/shard_map/all_gather | solution.py:126
  321.5 6.4 %convert_reduce_fusion = bf16[256,1024]{1,0:T(8,128)(2,1)S(1)} fusion(bf16[256,8,512]{0,2,1:T(8,128)(2,1)} %bitcast.84, bf16[1024,8,512]{0,2,1:T(8,128)(2,1)} %bitcast.83), kind=kOutput, calls=%fused_computation.17 | convolution fusion | flops 2151415808 | bytes 11010048 | tf_op jit(solution)/shard_map/sgc,fgc->gsf/dot_general | solution.py:132
  328.0 17.4 %all_to_all.56 = bf16[8,32,1024]{2,1,0:T(8,128)(2,1)S(1)} all-to-all(bf16[8,32,1024]{2,1,0:T(8,128)(2,1)S(1)} %bitcast.81), channel_id=1, replica_groups=mesh['section'=4,'tensor'=8] {'tensor'}, dimensions={0} | all-to-all | bytes 1048576 | tf_op jit(solution)/shard_map/all_to_all | solution.py:139
  345.3 0.4 reshape.100
  345.7 0.4 copy.67
  346.1 1.0 broadcast_in_dim_reshape.3
  (7 shorter events, 0.1 us)
Async XLA Ops:
  6.5 178.8 %all-gather.6.cloned.1.call-start = ((), (), s32[]{:S(2)}) async-start(), calls=%async_computation.3 | async-start | bytes 4718592 | tf_op jit(solution)/shard_map/all_gather | solution.py:77
  9.9 175.5 %all-gather.10.cloned.1.call-start = ((), (), s32[]{:S(2)}) async-start(), calls=%async_computation.5 | async-start | bytes 5242880 | tf_op jit(solution)/shard_map/all_gather | solution.py:97
  64.3 145.1 %all-gather.8.cloned.1.call-start = ((), (), s32[]{:S(2)}) async-start(), calls=%async_computation.4 | async-start | bytes 10485760 | tf_op jit(solution)/shard_map/all_gather | solution.py:96
  152.5 117.7 %all-gather.14.cloned.1.call-start = ((), (), s32[]{:S(2)}) async-start(), calls=%async_computation.7 | async-start | bytes 10485760 | tf_op jit(solution)/shard_map/all_gather | solution.py:124
  183.7 137.8 %all-gather.12.cloned.1.call-start = ((), (), s32[]{:S(2)}) async-start(), calls=%async_computation.6 | async-start | bytes 2359296 | tf_op jit(solution)/shard_map/all_gather | solution.py:126
Sparse Core Ops, SparseCore 0:
  10.0 100.8 all-gather.5
  112.4 34.0 all-gather.9
  152.6 56.7 all-gather.7
  210.8 59.4 all-gather.13
  272.2 49.2 all-gather.11
where the time goes:
time: 355 us; the launch traced here: 354 us
  blocking collectives  123 us (35%)
  waiting for transfers between devices  121 us (34%)
  local copies, waits for them, and re-layouts  51.8 us (15%)
  other arithmetic  22.6 us (6%)
  matrix products  21 us (6%)
  between operations  14 us (4%)
    all_to_all x1, blocking collectives, on_device(): lax.all_to_all(query_weight, 'tensor', split_axis=1, concat_axis=0, tiled...  55.8 us
    all_gather x1, waiting for transfers between devices, on_device(): out_rows = lax.all_gather(output_weight, 'section', axis=0, tiled=True)  51.3 us
    all_gather x1, waiting for transfers between devices, on_device(): piece = lax.all_gather(head_out, 'tensor', axis=1, tiled=True)  51.3 us
    all_to_all x1, blocking collectives, on_device(): lax.all_to_all(spread_heads, 'tensor', split_axis=1, concat_axis=0, tiled...  49.4 us
    unnamed x8, local copies, waits for them, and re-layouts  45.3 us
    all_gather x1, waiting for transfers between devices, on_device(): query_rows = lax.all_gather(query_slice, 'section', axis=0, tiled=True)  18.7 us
    convert_element_type x3, other arithmetic, adam_update(): (current - learn_rate * (corrected / denominator + decay_rate * current))...  18.6 us
    all_to_all x1, blocking collectives, on_device(): lax.all_to_all(feature_part, 'tensor', split_axis=0, concat_axis=1, tiled...  17.4 us
  transfers between devices with their start and end apart: 5, of which 3 were waited for; matrix products, arithmetic and copies ran while one was open for 23% of the time, Pallas kernels for 0%

commit v1 on v0

v1 whole, which is shorter than its diff:
```python
import math

import jax
import jax.numpy as jnp
from jax import lax
from jax.sharding import Mesh, PartitionSpec as P

QUERY_HEADS_LOCAL = 32
KEYVAL_HEADS = 4
HEAD_DIMENSION = 128


learn_rate = 0.015
beta_one = 0.5
beta_two = 0.9
adam_step = 1000.0
adam_eps = 1e-08
decay_rate = 0.1
norm_eps = 1e-06
rope_base = 1000000.0
masked_score = -1e30


def adam_update(current, gradient, moment, second):
    moment_new = beta_one * moment + (1.0 - beta_one) * gradient
    second_new = beta_two * second + (1.0 - beta_two) * gradient * gradient
    corrected = moment_new / (1.0 - beta_one**adam_step)
    denominator = jnp.sqrt(second_new / (1.0 - beta_two**adam_step)) + adam_eps
    return (current - learn_rate * (corrected / denominator + decay_rate * current)).astype(
        jnp.bfloat16
    )


def normalize(hidden, norm_gain):
    values = hidden.astype(jnp.float32)
    factor = lax.rsqrt(jnp.mean(values * values, axis=-1, keepdims=True) + norm_eps)
    return (values * factor * norm_gain).astype(jnp.bfloat16)


def rotary_embed(values, token_positions):
    half_width = values.shape[-1] // 2
    frequency = rope_base ** (-jnp.arange(half_width, dtype=jnp.float32) * 2.0 / values.shape[-1])
    angles = token_positions.astype(jnp.float32)[:, None] * frequency[None, :]
    cosine_table = jnp.concatenate([jnp.cos(angles), jnp.cos(angles)], axis=-1)
    sine_table = jnp.concatenate([jnp.sin(angles), jnp.sin(angles)], axis=-1)
    first_half = values[..., :half_width]
    second_half = values[..., half_width:]
    rotated = jnp.concatenate([-second_half, first_half], axis=-1)
    return values * cosine_table + rotated * sine_table


def on_device(
    hidden,
    norm_gain,
    lengths,
    query_param,
    query_grad,
    query_moment,
    query_second,
    keyval_param,
    keyval_gradient,
    keyval_first_moment,
    keyval_second_moment,
    output_param,
    output_grad,
    output_moment,
    output_second,
):
    sections = lax.axis_size("section")
    planes = lax.axis_size("plane")
    lanes = lax.axis_size("lane")
    members = sections * lanes
    group = ("section", "lane")
    rows = query_param.shape[0]
    head_columns = query_param.shape[1] // members
    heads_here = head_columns // HEAD_DIMENSION
    tokens_here, model_width = hidden.shape[1:]
    sequence = tokens_here * planes * lanes

    query_weight = adam_update(query_param, query_grad, query_moment, query_second)
    keyval_matrix = adam_update(
        keyval_param, keyval_gradient, keyval_first_moment, keyval_second_moment
    )
    output_weight = adam_update(output_param, output_grad, output_moment, output_second)

    spread_heads = jnp.repeat(
        keyval_matrix.reshape(rows, 2, KEYVAL_HEADS, HEAD_DIMENSION),
        members // KEYVAL_HEADS,
        axis=2,
    )
    spread_heads = spread_heads.transpose(2, 0, 1, 3).reshape(members, rows, 2 * HEAD_DIMENSION)
    query_pieces = query_weight.reshape(rows, members, head_columns).transpose(1, 0, 2)
    output_pieces = output_weight.reshape(rows, members, head_columns).transpose(1, 0, 2)
    query_rows = lax.all_to_all(query_pieces, group, 0, 0, tiled=True)
    keyval_rows = lax.all_to_all(spread_heads, group, 0, 0, tiled=True)
    output_rows = lax.all_to_all(output_pieces, group, 0, 0, tiled=True)
    query_rows = query_rows.reshape(members * rows, head_columns)
    keyval_rows = keyval_rows.reshape(members * rows, 2 * HEAD_DIMENSION)
    output_rows = output_rows.reshape(members * rows, head_columns)

    local_rows = normalize(hidden[0], norm_gain)
    features = local_rows.reshape(tokens_here, sections, planes, lanes * rows)
    features = features.transpose(2, 0, 1, 3).reshape(planes, tokens_here, members * rows)
    features = lax.all_to_all(features, "plane", 0, 0, tiled=True)
    normed = lax.all_gather(features, group, axis=0, tiled=True)
    normed = normed.reshape(sections * sequence, members * rows)

    partial = jnp.concatenate(
        [
            jnp.dot(normed, query_rows, preferred_element_type=jnp.float32).astype(jnp.bfloat16),
            jnp.dot(normed, keyval_rows, preferred_element_type=jnp.float32).astype(jnp.bfloat16),
        ],
        axis=1,
    ).reshape(sections, sequence, head_columns + 2 * HEAD_DIMENSION)
    partial = lax.all_to_all(partial, "plane", 0, 0, tiled=True)
    total = jnp.sum(partial.astype(jnp.float32), axis=0)

    order = jnp.arange(sequence).reshape(planes, lanes, tokens_here)
    token_positions = order.transpose(1, 0, 2).reshape(sequence)
    length = lax.dynamic_index_in_dim(
        lax.all_gather(lengths, "section", axis=0, tiled=True), lax.axis_index("plane"), 0, False
    )
    query_heads = rotary_embed(
        total[:, :head_columns].reshape(sequence, heads_here, HEAD_DIMENSION).transpose(1, 0, 2),
        token_positions,
    ).astype(jnp.bfloat16)
    key_head_rows = rotary_embed(
        total[:, head_columns : head_columns + HEAD_DIMENSION], token_positions
    ).astype(jnp.bfloat16)
    value_head_rows = total[:, head_columns + HEAD_DIMENSION :].astype(jnp.bfloat16)
    scores = jnp.einsum(
        "hqd,kd->hqk", query_heads, key_head_rows, preferred_element_type=jnp.float32
    ) / math.sqrt(HEAD_DIMENSION)
    allowed = (token_positions[None, :] <= token_positions[:, None]) & (
        token_positions[None, :] < length
    )
    scores = jnp.where(allowed[None], scores, masked_score)
    row_max = jnp.max(scores, axis=-1, keepdims=True)
    exponent = jnp.exp(scores - row_max)
    attention = (exponent / jnp.sum(exponent, axis=-1, keepdims=True)).astype(jnp.bfloat16)
    head_out = jnp.einsum(
        "hqk,kd->hqd", attention, value_head_rows, preferred_element_type=jnp.float32
    ).astype(jnp.bfloat16)
    head_out = head_out.transpose(1, 0, 2).reshape(sequence, head_columns)

    all_heads = lax.all_gather(head_out, "plane", axis=0, tiled=True)
    feature_part = lax.dot_general(
        all_heads, output_rows, (((1,), (1,)), ((), ())), preferred_element_type=jnp.float32
    ).astype(jnp.bfloat16)
    feature_part = feature_part.reshape(members, planes * tokens_here, members * rows)
    feature_part = lax.all_to_all(feature_part, group, 0, 0, tiled=True)
    summed = jnp.sum(feature_part.astype(jnp.float32), axis=0).astype(jnp.bfloat16)
    arrived = lax.all_to_all(
        summed.reshape(planes, tokens_here, members * rows), "plane", 0, 0, tiled=True
    )
    ordered = arrived.reshape(planes, tokens_here, sections, lanes * rows).transpose(1, 2, 0, 3)
    return ordered.reshape(1, tokens_here, model_width)


def solution(mesh):
    sections, tensors = mesh.shape["section"], mesh.shape["tensor"]
    lanes = tensors // sections
    grid = Mesh(
        mesh.devices.reshape(sections, tensors // lanes, lanes), ("section", "plane", "lane")
    )
    row_spec = P(("section", "plane", "lane"), None)
    token_spec = P("section", ("plane", "lane"), None)
    return jax.shard_map(
        on_device,
        mesh=grid,
        in_specs=(token_spec, P(), P("section")) + (row_spec,) * 12,
        out_specs=token_spec,
        check_vma=False,
    )
```

time: 355 us -> 293 us (0.83)
  waiting for transfers between devices: 121 us -> 52.2 us
  blocking collectives: 123 us -> 95.6 us
  starting transfers between devices: 0.35 us -> 15.4 us
  local copies, waits for them, and re-layouts: 51.8 us -> 66.7 us
  other arithmetic: 22.6 us -> 29 us
    all_gather x5 -> x2, waiting for transfers between devices: 121 us -> 16.8 us  [the longest x1 16.8 us: on_device(): all_heads = lax.all_gather(head_out, 'plane', axis=0, tiled=True)]
    all_to_all x0 -> x4, waiting for transfers between devices: none -> 35.4 us  [the longest x1 22.5 us: on_device(): query_rows = lax.all_to_all(query_pieces, group, 0, 0, tiled=True)]
    all_to_all x3, blocking collectives: 123 us -> 90.8 us  [the longest x1 51.4 us: on_device(): feature_part = lax.all_to_all(feature_part, group, 0, 0, tiled=True)]
    all_to_all x0 -> x4, starting transfers between devices: none -> 15.3 us  [the longest x1 4.44 us: on_device(): query_rows = lax.all_to_all(query_pieces, group, 0, 0, tiled=True)]
    dot_general x3, matrix products: 18.7 us -> 11 us  [the longest x1 5.36 us: on_device(): jnp.dot(normed, query_rows, preferred_element_type=jnp.float32)]
    unnamed x0 -> x1, blocking collectives: none -> 4.78 us
    reduce_sum x0 -> x2, other arithmetic: none -> 4.66 us  [the longest x1 2.95 us: on_device(): jnp.sum(feature_part.astype(jnp.float32), axis=0).astype(jnp.bfloat16)]
    reshape x4 -> x8, local copies, waits for them, and re-layouts: 1.18 us -> 5.19 us  [the longest x1 1.26 us: on_device(): partial = jnp.concatenate([jnp.dot(normed, query_rows, preferred_element_...]
  transfers between devices with their start and end apart: 5 -> 6, of which waited for: 3 -> 3; matrix products, arithmetic and copies ran while one was open for 23% -> 31% of each run, Pallas kernels for 0% -> 0%
where the time goes in v1:
time: 293 us; the launch traced here: 291 us
  blocking collectives  95.6 us (33%)
  local copies, waits for them, and re-layouts  66.7 us (23%)
  waiting for transfers between devices  52.2 us (18%)
  other arithmetic  29 us (10%)
  matrix products  18.1 us (6%)
  starting transfers between devices  15.4 us (5%)
  between operations  14.3 us (5%)
    all_to_all x1, blocking collectives, on_device(): feature_part = lax.all_to_all(feature_part, group, 0, 0, tiled=True)  51.4 us
    unnamed x25, local copies, waits for them, and re-layouts  48.3 us
    all_to_all x1, waiting for transfers between devices, on_device(): query_rows = lax.all_to_all(query_pieces, group, 0, 0, tiled=True)  22.5 us
    all_to_all x1, blocking collectives, on_device(): features = lax.all_to_all(features, 'plane', 0, 0, tiled=True)  20.7 us
    convert_element_type x3, other arithmetic, adam_update(): (current - learn_rate * (corrected / denominator + decay_rate * current))...  19.8 us
    all_to_all x1, blocking collectives, on_device(): lax.all_to_all(summed.reshape(planes, tokens_here, members * rows), 'plan...  18.6 us
    all_gather x1, waiting for transfers between devices, on_device(): all_heads = lax.all_gather(head_out, 'plane', axis=0, tiled=True)  16.8 us
    all_to_all x1, waiting for transfers between devices, on_device(): output_rows = lax.all_to_all(output_pieces, group, 0, 0, tiled=True)  12.9 us
  transfers between devices with their start and end apart: 6, of which 3 were waited for; matrix products, arithmetic and copies ran while one was open for 31% of the time, Pallas kernels for 0%

profile of v1, /device:TPU:0, one launch (start us, length us, event | category | flops | bytes accessed | tf_op | source)
XLA Modules:
  0.0 291.3 jit_solution(10280425736148397035)
XLA Ops:
  6.5 2.0 reshape.296
  8.5 1.3 multiply_reduce_fusion
  9.8 0.8 mul.153
  10.6 0.5 fusion.30
  11.1 0.4 reshape.279
  11.5 20.7 %all_to_all.35 = bf16[4,32,2048]{2,1,0:T(8,128)(2,1)} all-to-all(bf16[4,32,2048]{2,1,0:T(8,128)(2,1)S(1)} %reshape.279), channel_id=1, replica_groups=mesh['section'=4,'plane'=4,'lane'=2] {'plane'}, dimensions={0} | all-to-all | bytes 1048576 | tf_op jit(solution)/shard_map/all_to_all | solution.py:104
  32.2 0.0 all-gather.3.cloned.1.call-update
  32.3 2.6 fusion.29
  34.8 0.4 reshape.283
  35.2 0.3 copy.64
  35.5 1.1 broadcast_in_dim.11
  36.6 3.7 %all-to-all-start.2 = ((bf16[8,256,256]{1,2,0:T(8,128)(2,1)}), bf16[8,256,256]{1,2,0:T(8,128)(2,1)S(1)}, u32[]{:S(2)}, u32[]{:S(2)}) async-start(bf16[8,256,256]{1,2,0:T(8,128)(2,1)} %bitcast.9), calls=%async_computation.2 | async-start | bytes 2097152 | tf_op jit(solution)/shard_map/all_to_all | solution.py:95
  40.3 5.6 %copy.56 = f32[256,4096]{0,1:T(8,128)} copy(f32[256,4096]{1,0:T(8,128)} %param.20) | data formatting | bytes 8388608 | tf_op args[5]
  45.9 5.6 %copy.57 = f32[256,4096]{0,1:T(8,128)} copy(f32[256,4096]{1,0:T(8,128)} %param.19) | data formatting | bytes 8388608 | tf_op args[4]
  51.5 5.6 %copy.58 = f32[256,4096]{0,1:T(8,128)} copy(f32[256,4096]{1,0:T(8,128)} %param.21) | data formatting | bytes 8388608 | tf_op args[6]
  57.1 5.6 %copy.62 = f32[256,4096]{0,1:T(8,128)} copy(f32[256,4096]{1,0:T(8,128)} %param.18) | data formatting | bytes 8388608 | tf_op args[3]
  62.8 9.0 %fusion.16 = bf16[256,4096]{0,1:T(8,128)(2,1)} fusion(f32[256,4096]{0,1:T(8,128)} %copy.62, f32[256,4096]{0,1:T(8,128)} %copy.57, f32[256,4096]{0,1:T(8,128)} %copy.58, f32[256,4096]{0,1:T(8,128)} %copy.56), kind=kLoop, calls=%fused_computation.18 | loop fusion | flops 13631488 | bytes 18874368 | tf_op jit(solution)/shard_map/convert_element_type | solution.py:29
  71.7 4.4 %all-to-all-start.1 = ((bf16[8,256,512]{1,2,0:T(8,128)(2,1)}), bf16[8,256,512]{1,2,0:T(8,128)(2,1)S(1)}, u32[]{:S(2)}, u32[]{:S(2)}) async-start(bf16[8,256,512]{1,2,0:T(8,128)(2,1)} %bitcast.5), calls=%async_computation.1 | async-start | bytes 4194304 | tf_op jit(solution)/shard_map/all_to_all | solution.py:94
  76.8 0.6 dynamic-slice
  77.4 0.8 dynamic-update-slice
  78.2 1.3 copy.65
  79.5 22.5 %all-to-all-done.1 = bf16[8,256,512]{1,2,0:T(8,128)(2,1)S(1)} async-done(((bf16[8,256,512]{1,2,0:T(8,128)(2,1)}), bf16[8,256,512]{1,2,0:T(8,128)(2,1)S(1)}, u32[]{:S(2)}, u32[]{:S(2)}) %all-to-all-start.1) | async-done | bytes 2097184 | tf_op jit(solution)/shard_map/all_to_all | solution.py:94
  102.0 2.4 copy.63
  104.4 5.4 %convolution_convert_fusion.1 = bf16[1024,512]{0,1:T(8,128)(2,1)S(1)} fusion(bf16[1024,2048]{1,0:T(8,128)(2,1)} %bitcast.69, bf16[2048,512]{1,0:T(8,128)(2,1)} %bitcast.64), kind=kOutput, calls=%fused_computation.25 | convolution fusion | flops 2148007936 | bytes 7340032 | tf_op jit(solution)/shard_map/dot_general | solution.py:110
  109.7 1.3 convolution_convert_fusion.2
  111.1 0.2 pad_maximum_fusion
  111.2 1.3 copy.93
  112.5 3.6 %all-to-all-start.3 = ((bf16[4,256,768]{1,2,0:T(8,128)(2,1)}), bf16[4,256,768]{1,2,0:T(8,128)(2,1)S(1)}, u32[]{:S(2)}, u32[]{:S(2)}) async-start(bf16[4,256,768]{1,2,0:T(8,128)(2,1)} %bitcast.58), calls=%async_computation.3 | async-start | bytes 3145728 | tf_op jit(solution)/shard_map/all_to_all | solution.py:115
  116.1 4.8 %all-reduce = s32[4]{0:T(128)S(1)} all-reduce(s32[4]{0:T(128)S(1)} %dynamic-update-slice), channel_id=1, replica_groups=mesh['section'=4,'plane'=4,'lane'=2] {'section'}, use_global_device_ids=true, to_apply=%add | all-reduce | flops 4 | bytes 32
  120.9 0.1 reshape.278
  121.0 0.3 multiply_cosine_fusion
  121.3 0.8 copy.68
  122.1 0.8 copy.69
  122.8 5.6 %copy.72 = f32[256,4096]{0,1:T(8,128)} copy(f32[256,4096]{1,0:T(8,128)} %param.28) | data formatting | bytes 8388608 | tf_op args[13]
  128.4 5.6 %copy.73 = f32[256,4096]{0,1:T(8,128)} copy(f32[256,4096]{1,0:T(8,128)} %param.27) | data formatting | bytes 8388608 | tf_op args[12]
  134.0 5.6 %copy.74 = f32[256,4096]{0,1:T(8,128)} copy(f32[256,4096]{1,0:T(8,128)} %param.29) | data formatting | bytes 8388608 | tf_op args[14]
  139.6 5.6 %copy.78 = f32[256,4096]{0,1:T(8,128)} copy(f32[256,4096]{1,0:T(8,128)} %param.26) | data formatting | bytes 8388608 | tf_op args[11]
  145.2 0.6 dynamic_slice.4
  145.8 0.6 broadcast_compare_fusion
  146.5 0.8 compare_and_fusion
  147.2 8.3 %fusion.15 = bf16[256,4096]{0,1:T(8,128)(2,1)} fusion(f32[256,4096]{0,1:T(8,128)} %copy.78, f32[256,4096]{0,1:T(8,128)} %copy.73, f32[256,4096]{0,1:T(8,128)} %copy.74, f32[256,4096]{0,1:T(8,128)} %copy.72), kind=kLoop, calls=%fused_computation.17 | loop fusion | flops 13631488 | bytes 18874368 | tf_op jit(solution)/shard_map/convert_element_type | solution.py:29
  155.5 1.2 copy-done
  156.7 3.6 %all-to-all-start.4 = ((bf16[8,256,512]{1,2,0:T(8,128)(2,1)}), bf16[8,256,512]{1,2,0:T(8,128)(2,1)S(1)}, u32[]{:S(2)}, u32[]{:S(2)}) async-start(bf16[8,256,512]{1,2,0:T(8,128)(2,1)} %bitcast.18), calls=%async_computation.4 | async-start | bytes 4194304 | tf_op jit(solution)/shard_map/all_to_all | solution.py:96
  160.3 0.0 all-gather.5.cloned.1.call-start
  160.3 1.7 convert_reduce_fusion
  162.0 0.8 slice.32
  162.9 0.7 slice_negate_fusion.1
  163.5 1.2 copy.67
  164.7 0.2 slice_negate_fusion
  165.0 0.8 copy-done.1
  165.8 0.2 copy-done.2
  165.9 2.5 fusion.19
  168.4 1.9 fusion.55
  170.3 2.7 convolution_convert_fusion.3
  173.0 12.9 %all-to-all-done.4 = bf16[8,256,512]{1,2,0:T(8,128)(2,1)S(1)} async-done(((bf16[8,256,512]{1,2,0:T(8,128)(2,1)}), bf16[8,256,512]{1,2,0:T(8,128)(2,1)S(1)}, u32[]{:S(2)}, u32[]{:S(2)}) %all-to-all-start.4) | async-done | bytes 2097184 | tf_op jit(solution)/shard_map/all_to_all | solution.py:96
  186.0 2.4 copy.79
  188.3 16.8 %all-gather.5.cloned.1.call-done = bf16[1024,512]{0,1:T(8,128)(2,1)} async-done(((bf16[256,512]{0,1:T(8,128)(2,1)}), bf16[1024,512]{0,1:T(8,128)(2,1)}) %all-gather.5.cloned.1.call-update) | async-done | bytes 1048592 | tf_op jit(solution)/shard_map/all_gather | solution.py:146
  205.1 4.3 %convolution_convert_fusion = bf16[1024,2048]{1,0:T(8,128)(2,1)S(1)} fusion(bf16[1024,512]{0,1:T(8,128)(2,1)} %all-gather.5.cloned.1.call-done, bf16[2048,512]{1,0:T(8,128)(2,1)} %bitcast.63), kind=kOutput, calls=%fused_computation.19 | convolution fusion | flops 2149580800 | bytes 7340032 | tf_op jit(solution)/shard_map/dot_general | solution.py:147
  209.5 51.4 %all_to_all.36 = bf16[8,128,2048]{2,1,0:T(8,128)(2,1)} all-to-all(bf16[8,128,2048]{2,1,0:T(8,128)(2,1)S(1)} %bitcast.61), channel_id=1, replica_groups=mesh['section'=4,'plane'=4,'lane'=2] {'section','lane'}, dimensions={0} | all-to-all | bytes 8388608 | tf_op jit(solution)/shard_map/all_to_all | solution.py:151
  260.9 3.0 %reduce_sum.42 = bf16[128,2048]{1,0:T(8,128)(2,1)S(1)} reduce(bf16[8,128,2048]{2,1,0:T(8,128)(2,1)} %all_to_all.36, bf16[]{:T(256)} %constant.55.clone.1), dimensions={0}, to_apply=%region_4.5 | reduce | flops 1835008 | bytes 4718594 | tf_op jit(solution)/shard_map/reduce_sum | solution.py:152
  263.8 18.6 %all_to_all.37 = bf16[4,32,2048]{2,1,0:T(8,128)(2,1)S(1)} all-to-all(bf16[4,32,2048]{2,1,0:T(8,128)(2,1)S(1)} %bitcast.62), channel_id=1, replica_groups=mesh['section'=4,'plane'=4,'lane'=2] {'plane'}, dimensions={0} | all-to-all | bytes 1048576 | tf_op jit(solution)/shard_map/all_to_all | solution.py:153
  282.5 0.4 reshape.294
  282.9 0.4 copy.80
  283.3 1.2 reshape.295
  (23 shorter events, 0.1 us)
Async XLA Ops:
  6.5 25.7 %copy-start.4 = (f32[256,1024]{1,0:T(8,128)S(1)}, f32[256,1024]{1,0:T(8,128)}, u32[]{:S(2)}) copy-start(f32[256,1024]{1,0:T(8,128)} %param.22) | copy-start | bytes 3145732
  6.5 97.8 %all-gather.3.cloned.1.call-start = ((), (), s32[]{:S(2)}) async-start(), calls=%async_computation.7 | async-start | bytes 4718592 | tf_op jit(solution)/shard_map/all_gather | solution.py:105
  36.6 35.1 %all-to-all-start.2 = ((bf16[8,256,256]{1,2,0:T(8,128)(2,1)}), bf16[8,256,256]{1,2,0:T(8,128)(2,1)S(1)}, u32[]{:S(2)}, u32[]{:S(2)}) async-start(bf16[8,256,256]{1,2,0:T(8,128)(2,1)} %bitcast.9), calls=%async_computation.2 | async-start | bytes 2097152 | tf_op jit(solution)/shard_map/all_to_all | solution.py:95
  71.7 5.1 %copy-start.6 = (u32[32]{0:T(128)S(1)}, u32[32]{0:T(128)}, u32[]{:S(2)}) copy-start(u32[32]{0:T(128)} %constant.60) | copy-start | bytes 388
  71.7 30.2 %all-to-all-start.1 = ((bf16[8,256,512]{1,2,0:T(8,128)(2,1)}), bf16[8,256,512]{1,2,0:T(8,128)(2,1)S(1)}, u32[]{:S(2)}, u32[]{:S(2)}) async-start(bf16[8,256,512]{1,2,0:T(8,128)(2,1)} %bitcast.5), calls=%async_computation.1 | async-start | bytes 4194304 | tf_op jit(solution)/shard_map/all_to_all | solution.py:94
  104.4 5.4 %copy-start.3 = (bf16[8,256,256]{2,1,0:T(8,128)(2,1)S(1)}, bf16[8,256,256]{2,1,0:T(8,128)(2,1)}, u32[]{:S(2)}) copy-start(bf16[8,256,256]{2,1,0:T(8,128)(2,1)} %copy.65) | copy-start | bytes 3145732
  104.4 5.4 %copy-start.5 = (bf16[32,32,2048]{2,1,0:T(8,128)(2,1)S(1)}, bf16[32,32,2048]{2,1,0:T(8,128)(2,1)}, u32[]{:S(2)}) copy-start(bf16[32,32,2048]{2,1,0:T(8,128)(2,1)} %all-gather.3.cloned.1.call-done) | copy-start | bytes 12582916
  112.5 43.0 %all-to-all-start.3 = ((bf16[4,256,768]{1,2,0:T(8,128)(2,1)}), bf16[4,256,768]{1,2,0:T(8,128)(2,1)S(1)}, u32[]{:S(2)}, u32[]{:S(2)}) async-start(bf16[4,256,768]{1,2,0:T(8,128)(2,1)} %bitcast.58), calls=%async_computation.3 | async-start | bytes 3145728 | tf_op jit(solution)/shard_map/all_to_all | solution.py:115
  155.5 1.2 copy-start
  156.7 29.3 %all-to-all-start.4 = ((bf16[8,256,512]{1,2,0:T(8,128)(2,1)}), bf16[8,256,512]{1,2,0:T(8,128)(2,1)S(1)}, u32[]{:S(2)}, u32[]{:S(2)}) async-start(bf16[8,256,512]{1,2,0:T(8,128)(2,1)} %bitcast.18), calls=%async_computation.4 | async-start | bytes 4194304 | tf_op jit(solution)/shard_map/all_to_all | solution.py:96
  160.3 44.9 %all-gather.5.cloned.1.call-start = ((), (), s32[]{:S(2)}) async-start(), calls=%async_computation.8 | async-start | bytes 1310720 | tf_op jit(solution)/shard_map/all_gather | solution.py:146
  165.0 0.8 copy-start.1
  165.0 1.0 copy-start.2
Sparse Core Ops, SparseCore 0:
  32.4 46.7 all-gather.2
  173.2 31.9 all-gather.4

commit v2 on v1

--- a/solution.py
+++ b/solution.py
@@ -1,8 +1,12 @@
+import functools
 import math
 
 import jax
 import jax.numpy as jnp
+import numpy as np
 from jax import lax
+from jax.experimental import pallas as pl
+from jax.experimental.pallas import tpu as pltpu
 from jax.sharding import Mesh, PartitionSpec as P
 
 QUERY_HEADS_LOCAL = 32
@@ -157,6 +161,536 @@
     return ordered.reshape(1, tokens_here, model_width)
 
 
+def rope_tables(positions):
+    half_width = HEAD_DIMENSION // 2
+    frequency = (
+        rope_base ** (-np.arange(half_width, dtype=np.float64) * 2.0 / HEAD_DIMENSION)
+    ).astype(np.float32)
+    angles = positions.astype(np.float32)[:, None] * frequency[None, :]
+    cosine, sine = np.cos(angles), np.sin(angles)
+    return (
+        np.concatenate([cosine, cosine], axis=-1).astype(np.float32),
+        np.concatenate([-sine, sine], axis=-1).astype(np.float32),
+    )
+
+
+def block_kernel(
+    sizes,
+    hidden,
+    norm_gain,
+    length,
+    cosine,
+    sine,
+    rows_at,
+    columns_at,
+    qp,
+    qg,
+    qm,
+    qs,
+    kp,
+    kg,
+    km,
+    ks,
+    op,
+    og,
+    om,
+    os_,
+    out,
+    fetched,
+    w_send,
+    w_all,
+    o_send,
+    o_all,
+    x_send,
+    normed,
+    part_send,
+    part_recv,
+    total,
+    heads,
+    pair_send,
+    pair_recv,
+    red_send,
+    red_recv,
+    z_send,
+    z_recv,
+    length_here,
+    fetch_sem,
+    local_sem,
+    w_ssem,
+    w_rsem,
+    o_ssem,
+    o_rsem,
+    x_ssem,
+    x_rsem,
+    g_ssem,
+    g_rsem,
+    f_ssem,
+    p_ssem,
+    p_rsem,
+    h_ssem,
+    h_rsem,
+    b_ssem,
+    b_rsem,
+    r_ssem,
+    r_rsem,
+    z_ssem,
+    z_rsem,
+    l_ssem,
+    l_rsem,
+):
+    S, NP, L = sizes
+    G = S * L
+    half = S // 2
+    s, p, l = lax.axis_index("section"), lax.axis_index("plane"), lax.axis_index("lane")
+    j = s * L + l
+    core = lax.rem(s, 2)
+    pair = s // 2
+    sibling = s + 1 - 2 * core
+    rows = qp.shape[0]
+    width = w_all.shape[2]
+    hc = width - 2 * HEAD_DIMENSION
+    tokens = hidden.shape[0]
+    strip = L * rows
+    seq = NP * tokens * L
+
+    def member(m):
+        return (m // L, p, lax.rem(m, L))
+
+    def at_plane(q):
+        return (s, q, l)
+
+    def remote(src, dst, ssem, rsem, device):
+        return pltpu.make_async_remote_copy(
+            src_ref=src,
+            dst_ref=dst,
+            send_sem=ssem,
+            recv_sem=rsem,
+            device_id=device,
+            device_id_type=pl.DeviceIdType.MESH,
+        )
+
+    same_core = []
+    for da in range(half):
+        for dl in range(L):
+            sec = 2 * lax.rem(pair + da, half) + core
+            lane = lax.rem(l + dl, L)
+            same_core.append((sec, lane))
+    others = same_core[1:]
+
+    barrier = pltpu.get_barrier_semaphore()
+    for d in range(1, G):
+        pl.semaphore_signal(
+            barrier, inc=1, device_id=member(lax.rem(j + d, G)), device_id_type=pl.DeviceIdType.MESH
+        )
+    for d in range(1, NP):
+        pl.semaphore_signal(
+            barrier,
+            inc=1,
+            device_id=at_plane(lax.rem(p + d, NP)),
+            device_id_type=pl.DeviceIdType.MESH,
+        )
+
+    def fetch(refs, kv_refs, i, slot):
+        dest = lax.rem(j + i, G)
+        head = dest // (G // KEYVAL_HEADS)
+        copies = []
+        for a, ref in enumerate(refs):
+            copies.append(
+                pltpu.make_async_copy(
+                    ref.at[:, pl.ds(pl.multiple_of(dest * hc, 128), hc)],
+                    fetched.at[slot, a, :, pl.ds(0, hc)],
+                    fetch_sem.at[slot, a, 0],
+                )
+            )
+        for a, ref in enumerate(kv_refs):
+            for part in range(2):
+                copies.append(
+                    pltpu.make_async_copy(
+                        ref.at[
+                            :,
+                            pl.ds(
+                                pl.multiple_of((part * KEYVAL_HEADS + head) * HEAD_DIMENSION, 128),
+                                HEAD_DIMENSION,
+                            ),
+                        ],
+                        fetched.at[slot, a, :, pl.ds(hc + part * HEAD_DIMENSION, HEAD_DIMENSION)],
+                        fetch_sem.at[slot, a, 1 + part],
+                    )
+                )
+        return copies
+
+    def update(slot, n_columns, dst, i):
+        @pl.loop(0, rows // 16)
+        def _(t):
+            r = pl.ds(pl.multiple_of(t * 16, 16), 16)
+            piece = [fetched[slot, a, r, 0:n_columns] for a in range(4)]
+            dst[i, r, :] = adam_update(*piece)
+
+    def update_all(refs, kv_refs, n_columns, dst, after):
+        @pl.loop(1, G + 1)
+        def _(i):
+            slot = lax.rem(i, 2)
+            for copy in fetch(refs, kv_refs, i, slot):
+                copy.wait()
+
+            @pl.when(i < G)
+            def _():
+                for copy in fetch(refs, kv_refs, i + 1, 1 - slot):
+                    copy.start()
+
+            update(slot, n_columns, dst, i - 1)
+            after(i)
+
+    for copy in fetch((qp, qg, qm, qs), (kp, kg, km, ks), 1, 1):
+        copy.start()
+
+    squares = jnp.zeros((tokens, 1), jnp.float32)
+    for c in range(S * NP):
+        v = hidden[:, c * strip : (c + 1) * strip].astype(jnp.float32)
+        squares += jnp.sum(v * v, axis=-1, keepdims=True)
+    factor = lax.rsqrt(squares / (S * NP * strip) + norm_eps)
+    for c in range(S * NP):
+        at = slice(c * strip, (c + 1) * strip)
+        v = hidden[:, at].astype(jnp.float32) * factor * norm_gain[0:1, at]
+        x_send[c % NP, :, (c // NP) * strip : (c // NP + 1) * strip] = v.astype(jnp.bfloat16)
+
+    pl.semaphore_wait(barrier, G - 1 + NP - 1)
+
+    @pl.when(s == p)
+    def _():
+        for d in range(1, S):
+            remote(
+                length, length_here, l_ssem.at[d], l_rsem, (lax.rem(s + d, S), p, l)
+            ).start()
+
+    def x_copy(q, src_plane, d):
+        return remote(
+            x_send.at[q], normed.at[j, src_plane], x_ssem.at[d], x_rsem.at[src_plane], at_plane(q)
+        )
+
+    for d in range(1, NP):
+        x_copy(lax.rem(p + d, NP), p, d).start()
+    own_x = pltpu.make_async_copy(x_send.at[p], normed.at[j, p], local_sem.at[0])
+    own_x.start()
+
+    def w_copy(i):
+        dest = lax.rem(j + i, G)
+        return remote(
+            w_send.at[i - 1], w_all.at[j], w_ssem.at[i - 1], w_rsem.at[j], member(dest)
+        )
+
+    def after_w(i):
+        @pl.when(i < G)
+        def _():
+            w_copy(i).start()
+
+    update_all((qp, qg, qm, qs), (kp, kg, km, ks), width, w_send, after_w)
+    own_w = pltpu.make_async_copy(w_send.at[G - 1], w_all.at[j], local_sem.at[1])
+    own_w.start()
+    for copy in fetch((op, og, om, os_), (), 1, 1):
+        copy.start()
+
+    for d in range(1, NP):
+        src_plane = lax.rem(p + d, NP)
+        remote(
+            x_send.at[src_plane],
+            normed.at[j, src_plane],
+            x_ssem.at[d],
+            x_rsem.at[src_plane],
+            at_plane(src_plane),
+        ).wait_recv()
+    own_x.wait()
+
+    def g_copy(block, ssem, device):
+        return remote(normed.at[block], normed.at[block], ssem, g_rsem.at[block], device)
+
+    for n, (sec, lane) in enumerate(others):
+        g_copy(j, g_ssem.at[n], (sec, p, lane)).start()
+    g_copy(j, f_ssem.at[0], (sibling, p, l)).start()
+
+    update_all((op, og, om, os_), (), hc, o_send, lambda i: None)
+
+    for n, (sec, lane) in enumerate(others):
+        block = sec * L + lane
+        g_copy(block, g_ssem.at[n], (sec, p, lane)).wait_recv()
+        g_copy(block, f_ssem.at[n + 1], (sibling, p, l)).start()
+    for d in range(1, G):
+        src = lax.rem(j + d, G)
+        remote(w_send.at[0], w_all.at[src], w_ssem.at[0], w_rsem.at[src], member(src)).wait_recv()
+    own_w.wait()
+    for n, (sec, lane) in enumerate(same_core):
+        block = (sec + 1 - 2 * core) * L + lane
+        g_copy(block, f_ssem.at[n], (sibling, p, l)).wait_recv()
+
+    def o_copy(i):
+        dest = lax.rem(j + i, G)
+        return remote(
+            o_send.at[i - 1], o_all.at[j], o_ssem.at[i - 1], o_rsem.at[j], member(dest)
+        )
+
+    for i in range(1, G):
+        o_copy(i).start()
+    own_o = pltpu.make_async_copy(o_send.at[G - 1], o_all.at[j], local_sem.at[2])
+    own_o.start()
+
+    def product(prompt):
+        x = normed[pl.ds(prompt * L, L)].reshape(seq, G * rows)
+        w = w_all[...].reshape(G * rows, width)
+        return jnp.dot(x, w, preferred_element_type=jnp.float32)
+
+    def p_copy(d):
+        q = lax.rem(p + d, NP)
+        return remote(
+            part_send.at[d - 1], part_recv.at[p], p_ssem.at[d - 1], p_rsem.at[p], at_plane(q)
+        )
+
+    @pl.loop(1, NP)
+    def _(d):
+        part_send[d - 1] = product(lax.rem(p + d, NP)).astype(jnp.bfloat16)
+        p_copy(d).start()
+
+    total[...] = product(p)
+    for d in range(1, NP):
+        q = lax.rem(p + d, NP)
+        remote(
+            part_send.at[0], part_recv.at[q], p_ssem.at[0], p_rsem.at[q], at_plane(q)
+        ).wait_recv()
+        total[...] += part_recv[q].astype(jnp.float32)
+
+    @pl.when(s == p)
+    def _():
+        length_here[...] = length[...]
+        for d in range(1, S):
+            remote(
+                length, length_here, l_ssem.at[d], l_rsem, (lax.rem(s + d, S), p, l)
+            ).wait_send()
+
+    @pl.when(s != p)
+    def _():
+        remote(length, length_here, l_ssem.at[0], l_rsem, (p, p, l)).wait_recv()
+
+    def rotate(x):
+        return (x * cosine[...] + pltpu.roll(x, HEAD_DIMENSION // 2, 1) * sine[...]).astype(
+            jnp.bfloat16
+        )
+
+    key_rows = rotate(total[:, hc : hc + HEAD_DIMENSION])
+    value_rows = total[:, hc + HEAD_DIMENSION :].astype(jnp.bfloat16)
+    limit = jnp.concatenate([length_here[0:1, :]] * (seq // 128), axis=1)
+    column = columns_at[0:1, :]
+    allowed = (column <= rows_at[...]) & (column < limit)
+    for h in range(hc // HEAD_DIMENSION):
+        at = slice(h * HEAD_DIMENSION, (h + 1) * HEAD_DIMENSION)
+        scores = lax.dot_general(
+            rotate(total[:, at]),
+            key_rows,
+            (((1,), (1,)), ((), ())),
+            preferred_element_type=jnp.float32,
+        ) / math.sqrt(HEAD_DIMENSION)
+        scores = jnp.where(allowed, scores, masked_score)
+        exponent = jnp.exp(scores - jnp.max(scores, axis=-1, keepdims=True))
+        attention = (exponent / jnp.sum(exponent, axis=-1, keepdims=True)).astype(jnp.bfloat16)
+        heads[p, :, at] = jnp.dot(
+            attention, value_rows, preferred_element_type=jnp.float32
+        ).astype(jnp.bfloat16)
+
+    for d in range(1, NP):
+        remote(
+            heads.at[p], heads.at[p], h_ssem.at[d], h_rsem.at[p], at_plane(lax.rem(p + d, NP))
+        ).start()
+
+    for d in range(1, G):
+        src = lax.rem(j + d, G)
+        remote(o_send.at[0], o_all.at[src], o_ssem.at[0], o_rsem.at[src], member(src)).wait_recv()
+    own_o.wait()
+
+    def heads_wait(q):
+        @pl.when(q != p)
+        def _():
+            remote(heads.at[q], heads.at[q], h_ssem.at[0], h_rsem.at[q], at_plane(q)).wait_recv()
+
+    def features(prompt, b):
+        return lax.dot_general(
+            heads[prompt], o_all[b], (((1,), (1,)), ((), ())), preferred_element_type=jnp.float32
+        )
+
+    def b_copy(e):
+        return remote(
+            pair_send.at[e], pair_recv.at[e], b_ssem.at[e], b_rsem.at[e], (sibling, p, l)
+        )
+
+    for e in range(half):
+        prompt = 2 * lax.rem(pair + e, half) + 1 - core
+        heads_wait(prompt)
+
+        @pl.loop(0, G)
+        def _(b):
+            at = pl.ds(pl.multiple_of(b * rows, 128), rows)
+            pair_send[e, :, at] = features(prompt, b).astype(jnp.bfloat16)
+
+        b_copy(e).start()
+
+    here = pair * L + l
+
+    def r_copy(da, dl, n):
+        sec, lane = same_core[da * L + dl]
+        return remote(
+            red_send.at[da, lane], red_recv.at[here], r_ssem.at[n], r_rsem.at[here], (sec, p, lane)
+        )
+
+    for e in list(range(1, half)) + [0]:
+        prompt = 2 * lax.rem(pair + e, half) + core
+        heads_wait(prompt)
+        b_copy(e).wait_recv()
+
+        @pl.loop(0, G)
+        def _(b):
+            at = pl.ds(pl.multiple_of(b * rows, 128), rows)
+            value = features(prompt, b) + pair_recv[e, :, at].astype(jnp.float32)
+            red_send[e, :, :, at] = value.astype(jnp.bfloat16).reshape(L, seq // L, rows)
+
+        for dl in range(L):
+            if e or dl:
+                r_copy(e, dl, e * L + dl).start()
+
+    summed = red_send[0, l].astype(jnp.float32)
+    for n in range(1, half * L):
+        sec, lane = same_core[n]
+        src = (sec // 2) * L + lane
+        remote(
+            red_send.at[0, l], red_recv.at[src], r_ssem.at[0], r_rsem.at[src], (sec, p, lane)
+        ).wait_recv()
+        summed += red_recv[src].astype(jnp.float32)
+    z_send[...] = summed.astype(jnp.bfloat16).reshape(NP, tokens, G * rows)
+
+    def z_copy(q, d):
+        return remote(z_send.at[q], z_recv.at[p], z_ssem.at[d], z_rsem.at[p], at_plane(q))
+
+    for d in range(1, NP):
+        z_copy(lax.rem(p + d, NP), d).start()
+    z_recv[p] = z_send[p]
+    for d in range(1, NP):
+        q = lax.rem(p + d, NP)
+        remote(z_send.at[q], z_recv.at[q], z_ssem.at[d], z_rsem.at[q], at_plane(q)).wait_recv()
+    for c in range(S * NP):
+        out[:, c * strip : (c + 1) * strip] = z_recv[
+            c % NP, :, (c // NP) * strip : (c // NP + 1) * strip
+        ]
+
+    for d in range(1, NP):
+        q = lax.rem(p + d, NP)
+        x_copy(q, p, d).wait_send()
+        p_copy(d).wait_send()
+        remote(heads.at[p], heads.at[p], h_ssem.at[d], h_rsem.at[p], at_plane(q)).wait_send()
+        z_copy(q, d).wait_send()
+    for i in range(1, G):
+        w_copy(i).wait_send()
+        o_copy(i).wait_send()
+    for n, (sec, lane) in enumerate(others):
+        g_copy(j, g_ssem.at[n], (sec, p, lane)).wait_send()
+    for n, (sec, lane) in enumerate(same_core):
+        g_copy(sec * L + lane, f_ssem.at[n], (sibling, p, l)).wait_send()
+    for e in range(half):
+        b_copy(e).wait_send()
+    for n in range(1, half * L):
+        r_copy(n // L, n % L, n).wait_send()
+
+
+def fused(hidden, norm_gain, lengths, *weights):
+    S, NP, L = (lax.axis_size(a) for a in ("section", "plane", "lane"))
+    G = S * L
+    half = S // 2
+    rows = weights[0].shape[0]
+    hc = weights[0].shape[1] // G
+    width = hc + 2 * HEAD_DIMENSION
+    tokens = hidden.shape[1]
+    seq = tokens * NP * L
+    order = np.arange(seq).reshape(NP, L, tokens).transpose(1, 0, 2).reshape(seq)
+    cosine, sine = rope_tables(order)
+    rows_at = np.broadcast_to(order.astype(np.int32)[:, None], (seq, seq))
+    columns_at = np.broadcast_to(order.astype(np.int32)[None, :], (8, seq))
+    length = jnp.broadcast_to(lengths[:, None], (8, 128))
+    bf, f32 = jnp.bfloat16, jnp.float32
+    dma = pltpu.SemaphoreType.DMA
+    vmem = pl.BlockSpec(memory_space=pltpu.VMEM)
+    hbm = pl.BlockSpec(memory_space=pl.ANY)
+    scratch = [
+        pltpu.VMEM((2, 4, rows, width), f32),
+        pltpu.VMEM((G, rows, width), bf),
+        pltpu.VMEM((G, rows, width), bf),
+        pltpu.VMEM((G, rows, hc), bf),
+        pltpu.VMEM((G, rows, hc), bf),
+        pltpu.VMEM((NP, tokens, G * rows), bf),
+        pltpu.VMEM((G, NP, tokens, G * rows), bf),
+        pltpu.VMEM((NP - 1, seq, width), bf),
+        pltpu.VMEM((NP, seq, width), bf),
+        pltpu.VMEM((seq, width), f32),
+        pltpu.VMEM((NP, seq, hc), bf),
+        pltpu.VMEM((half, seq, G * rows), bf),
+        pltpu.VMEM((half, seq, G * rows), bf),
+        pltpu.VMEM((half, L, seq // L, G * rows), bf),
+        pltpu.VMEM((half * L, seq // L, G * rows), bf),
+        pltpu.VMEM((NP, tokens, G * rows), bf),
+        pltpu.VMEM((NP, tokens, G * rows), bf),
+        pltpu.VMEM((8, 128), jnp.int32),
+        dma((2, 4, 3)),
+        dma((3,)),
+        dma((G,)),
+        dma((G,)),
+        dma((G,)),
+        dma((G,)),
+        dma((NP,)),
+        dma((NP,)),
+        dma((half * L,)),
+        dma((G,)),
+        dma((half * L,)),
+        dma((NP,)),
+        dma((NP,)),
+        dma((NP,)),
+        dma((NP,)),
+        dma((half,)),
+        dma((half,)),
+        dma((half * L,)),
+        dma((half * L,)),
+        dma((NP,)),
+        dma((NP,)),
+        dma((S,)),
+        dma,
+    ]
+    result = pl.pallas_call(
+        functools.partial(block_kernel, (S, NP, L)),
+        out_shape=jax.ShapeDtypeStruct(hidden.shape[1:], bf),
+        in_specs=[vmem] * 7 + [hbm] * 12,
+        out_specs=vmem,
+        scratch_shapes=scratch,
+        compiler_params=pltpu.CompilerParams(
+            collective_id=0, has_side_effects=True, vmem_limit_bytes=58 * 2**20
+        ),
+        cost_estimate=pl.CostEstimate(
+            flops=8 * 10**9, bytes_accessed=4 * 10**7, transcendentals=10**6
+        ),
+    )(
+        hidden[0],
+        norm_gain[None, :],
+        length,
+        jnp.asarray(cosine),
+        jnp.asarray(sine),
+        jnp.asarray(rows_at),
+        jnp.asarray(columns_at),
+        *weights,
+    )
+    return result[None]
+
+
+def layer(hidden, norm_gain, lengths, *weights):
+    whole_tiles = (
+        hidden.shape[1] % 16 == 0
+        and weights[0].shape[0] % 128 == 0
+        and lax.axis_size("section") % 2 == 0
+    )
+    return (fused if whole_tiles else on_device)(hidden, norm_gain, lengths, *weights)
+
+
 def solution(mesh):
     sections, tensors = mesh.shape["section"], mesh.shape["tensor"]
     lanes = tensors // sections
@@ -166,7 +700,7 @@
     row_spec = P(("section", "plane", "lane"), None)
     token_spec = P("section", ("plane", "lane"), None)
     return jax.shard_map(
-        on_device,
+        layer,
         mesh=grid,
         in_specs=(token_spec, P(), P("section")) + (row_spec,) * 12,
         out_specs=token_spec,

time: 293 us -> 179 us (0.61)
  the two profiles are of different devices: /device:TPU:0 before, /device:TPU:17 now
where the time goes in v2:
time: 179 us; the launch traced here: 178 us
  Pallas kernels  173 us (97%)
  local copies, waits for them, and re-layouts  5.21 us (3%)
    pallas_call x1, Pallas kernels, fused(): pl.pallas_call(functools.partial(block_kernel, (S, NP, L)), out_shape=jax...  173 us

profile of v2, /device:TPU:17, one launch (start us, length us, event | category | flops | bytes accessed | tf_op | source)
XLA Modules:
  0.0 178.5 jit_solution(7792180186514079734)
XLA Ops:
  0.7 0.6 broadcast_in_dim.16.length
  1.2 1.3 jit_solution_.7.columns_at
  2.5 1.5 jit_solution_.6.rows_at
  4.0 172.6 %shard_map.181 = bf16[32,8192]{1,0:T(8,128)(2,1)} custom-call(bf16[32,8192]{1,0:T(8,128)(2,1)} %bitcast.6, f32[1,8192]{1,0:T(1,128)} %bitcast.7, s32[8,128]{1,0:T(8,128)} %broadcast_in_dim.16.length, f32[256,128]{1,0:T(8,128)} %constant.6.clone.cosine, f32[256,128]{1,0:T(8,128)} %constant.7.clone.sine, s32[256,256]{1,0:T(8,128)} %jit_solution_.6.rows_at, ...), custom_call_target="tpu_custom_call" | custom-call | flops 8000000000 | bytes 40000000 | tf_op jit(solution)/shard_map/pallas_call | solution.py:660
  176.6 1.9 %copy.22 = bf16[1,32,8192]{2,1,0:T(8,128)(2,1)} copy(bf16[1,32,8192]{2,1,0:T(8,128)(2,1)} %bitcast.5) | data formatting | bytes 1048576

commit v3 on v2

--- a/solution.py
+++ b/solution.py
@@ -178,11 +178,9 @@
     sizes,
     hidden,
     norm_gain,
-    length,
+    lengths,
     cosine,
     sine,
-    rows_at,
-    columns_at,
     qp,
     qg,
     qm,
@@ -197,25 +195,35 @@
     os_,
     out,
     fetched,
+    a_send,
+    a_all,
     w_send,
     w_all,
     o_send,
     o_all,
     x_send,
     normed,
-    part_send,
-    part_recv,
-    total,
-    heads,
+    pa_send,
+    pa_recv,
+    pb_send,
+    pb_recv,
+    total_a,
+    total_b,
+    keyval,
+    heads_a,
+    heads_b,
     pair_send,
     pair_recv,
     red_send,
     red_recv,
     z_send,
     z_recv,
+    length,
     length_here,
     fetch_sem,
     local_sem,
+    a_ssem,
+    a_rsem,
     w_ssem,
     w_rsem,
     o_ssem,
@@ -225,10 +233,16 @@
     g_ssem,
     g_rsem,
     f_ssem,
-    p_ssem,
-    p_rsem,
-    h_ssem,
-    h_rsem,
+    pa_ssem,
+    pa_rsem,
+    pb_ssem,
+    pb_rsem,
+    k_ssem,
+    k_rsem,
+    ha_ssem,
+    ha_rsem,
+    hb_ssem,
+    hb_rsem,
     b_ssem,
     b_rsem,
     r_ssem,
@@ -247,8 +261,9 @@
     pair = s // 2
     sibling = s + 1 - 2 * core
     rows = qp.shape[0]
-    width = w_all.shape[2]
-    hc = width - 2 * HEAD_DIMENSION
+    split = w_all.shape[2]
+    first = a_all.shape[2] - HEAD_DIMENSION
+    hc = first + split
     tokens = hidden.shape[0]
     strip = L * rows
     seq = NP * tokens * L
@@ -276,6 +291,8 @@
             lane = lax.rem(l + dl, L)
             same_core.append((sec, lane))
     others = same_core[1:]
+
+    length[...] = jnp.full(length.shape, lengths[0], jnp.int32)
 
     barrier = pltpu.get_barrier_semaphore()
     for d in range(1, G):
@@ -290,58 +307,63 @@
             device_id_type=pl.DeviceIdType.MESH,
         )
 
-    def fetch(refs, kv_refs, i, slot):
+    def fetch(refs, kv_refs, begin, n_columns, i, slot):
         dest = lax.rem(j + i, G)
-        head = dest // (G // KEYVAL_HEADS)
+        sec, lane = dest // L, lax.rem(dest, L)
+        chip = (sec // 2) * L + lane
+        block = chip * 2 + lax.rem(sec, 2)
         copies = []
         for a, ref in enumerate(refs):
             copies.append(
                 pltpu.make_async_copy(
-                    ref.at[:, pl.ds(pl.multiple_of(dest * hc, 128), hc)],
-                    fetched.at[slot, a, :, pl.ds(0, hc)],
+                    ref.at[:, pl.ds(pl.multiple_of(block * hc + begin, 128), n_columns)],
+                    fetched.at[slot, a, :, pl.ds(0, n_columns)],
                     fetch_sem.at[slot, a, 0],
                 )
             )
         for a, ref in enumerate(kv_refs):
-            for part in range(2):
-                copies.append(
-                    pltpu.make_async_copy(
-                        ref.at[
-                            :,
-                            pl.ds(
-                                pl.multiple_of((part * KEYVAL_HEADS + head) * HEAD_DIMENSION, 128),
-                                HEAD_DIMENSION,
-                            ),
-                        ],
-                        fetched.at[slot, a, :, pl.ds(hc + part * HEAD_DIMENSION, HEAD_DIMENSION)],
-                        fetch_sem.at[slot, a, 1 + part],
-                    )
+            head = lax.rem(sec, 2) * KEYVAL_HEADS + chip
+            copies.append(
+                pltpu.make_async_copy(
+                    ref.at[:, pl.ds(pl.multiple_of(head * HEAD_DIMENSION, 128), HEAD_DIMENSION)],
+                    fetched.at[slot, a, :, pl.ds(n_columns, HEAD_DIMENSION)],
+                    fetch_sem.at[slot, a, 1],
                 )
+            )
         return copies
 
-    def update(slot, n_columns, dst, i):
-        @pl.loop(0, rows // 16)
-        def _(t):
-            r = pl.ds(pl.multiple_of(t * 16, 16), 16)
-            piece = [fetched[slot, a, r, 0:n_columns] for a in range(4)]
-            dst[i, r, :] = adam_update(*piece)
-
-    def update_all(refs, kv_refs, n_columns, dst, after):
+    def update_all(job, following, n_columns, dst, after):
         @pl.loop(1, G + 1)
         def _(i):
             slot = lax.rem(i, 2)
-            for copy in fetch(refs, kv_refs, i, slot):
+            for copy in fetch(*job, i, slot):
                 copy.wait()
 
             @pl.when(i < G)
             def _():
-                for copy in fetch(refs, kv_refs, i + 1, 1 - slot):
+                for copy in fetch(*job, i + 1, 1 - slot):
                     copy.start()
 
-            update(slot, n_columns, dst, i - 1)
+            if following is not None:
+
+                @pl.when(i == G)
+                def _():
+                    for copy in fetch(*following, 1, 1):
+                        copy.start()
+
+            @pl.loop(0, rows // 16)
+            def _(t):
+                r = pl.ds(pl.multiple_of(t * 16, 16), 16)
+                piece = [fetched[slot, a, r, 0:n_columns] for a in range(4)]
+                dst[i - 1, r, :] = adam_update(*piece)
+
             after(i)
 
-    for copy in fetch((qp, qg, qm, qs), (kp, kg, km, ks), 1, 1):
+    query_refs, keyval_refs = (qp, qg, qm, qs), (kp, kg, km, ks)
+    job_a = (query_refs, keyval_refs, 0, first)
+    job_w = (query_refs, (), first, split)
+    job_o = ((op, og, om, os_), (), 0, hc)
+    for copy in fetch(*job_a, 1, 1):
         copy.start()
 
     squares = jnp.zeros((tokens, 1), jnp.float32)
@@ -373,22 +395,40 @@
     own_x = pltpu.make_async_copy(x_send.at[p], normed.at[j, p], local_sem.at[0])
     own_x.start()
 
-    def w_copy(i):
-        dest = lax.rem(j + i, G)
-        return remote(
-            w_send.at[i - 1], w_all.at[j], w_ssem.at[i - 1], w_rsem.at[j], member(dest)
-        )
-
-    def after_w(i):
+    def weight_copies(send, gathered, ssem, rsem):
+        def copy(i):
+            return remote(
+                send.at[i - 1],
+                gathered.at[j],
+                ssem.at[i - 1],
+                rsem.at[j],
+                member(lax.rem(j + i, G)),
+            )
+
+        return copy
+
+    def weight_wait(send, gathered, ssem, rsem):
+        for d in range(1, G):
+            src = lax.rem(j + d, G)
+            remote(
+                send.at[0], gathered.at[src], ssem.at[0], rsem.at[src], member(src)
+            ).wait_recv()
+
+    a_copy = weight_copies(a_send, a_all, a_ssem, a_rsem)
+    w_copy = weight_copies(w_send, w_all, w_ssem, w_rsem)
+    o_copy = weight_copies(o_send, o_all, o_ssem, o_rsem)
+
+    def after_a(i):
         @pl.when(i < G)
         def _():
-            w_copy(i).start()
-
-    update_all((qp, qg, qm, qs), (kp, kg, km, ks), width, w_send, after_w)
-    own_w = pltpu.make_async_copy(w_send.at[G - 1], w_all.at[j], local_sem.at[1])
+            a_copy(i).start()
+
+    update_all(job_a, job_w, first + HEAD_DIMENSION, a_send, after_a)
+    own_a = pltpu.make_async_copy(a_send.at[G - 1], a_all.at[j], local_sem.at[1])
+    own_a.start()
+    update_all(job_w, job_o, split, w_send, lambda i: None)
+    own_w = pltpu.make_async_copy(w_send.at[G - 1], w_all.at[j], local_sem.at[2])
     own_w.start()
-    for copy in fetch((op, og, om, os_), (), 1, 1):
-        copy.start()
 
     for d in range(1, NP):
         src_plane = lax.rem(p + d, NP)
@@ -408,54 +448,52 @@
         g_copy(j, g_ssem.at[n], (sec, p, lane)).start()
     g_copy(j, f_ssem.at[0], (sibling, p, l)).start()
 
-    update_all((op, og, om, os_), (), hc, o_send, lambda i: None)
+    update_all(job_o, None, hc, o_send, lambda i: None)
+    own_o = pltpu.make_async_copy(o_send.at[G - 1], o_all.at[j], local_sem.at[3])
+    own_o.start()
 
     for n, (sec, lane) in enumerate(others):
         block = sec * L + lane
         g_copy(block, g_ssem.at[n], (sec, p, lane)).wait_recv()
         g_copy(block, f_ssem.at[n + 1], (sibling, p, l)).start()
-    for d in range(1, G):
-        src = lax.rem(j + d, G)
-        remote(w_send.at[0], w_all.at[src], w_ssem.at[0], w_rsem.at[src], member(src)).wait_recv()
-    own_w.wait()
+    for i in range(1, G):
+        w_copy(i).start()
+    weight_wait(a_send, a_all, a_ssem, a_rsem)
+    own_a.wait()
     for n, (sec, lane) in enumerate(same_core):
         block = (sec + 1 - 2 * core) * L + lane
         g_copy(block, f_ssem.at[n], (sibling, p, l)).wait_recv()
 
-    def o_copy(i):
-        dest = lax.rem(j + i, G)
-        return remote(
-            o_send.at[i - 1], o_all.at[j], o_ssem.at[i - 1], o_rsem.at[j], member(dest)
-        )
-
+    def product(prompt, weight):
+        x = normed[pl.ds(prompt * L, L)].reshape(seq, G * rows)
+        w = weight[...].reshape(G * rows, weight.shape[2])
+        return jnp.dot(x, w, preferred_element_type=jnp.float32)
+
+    def part_copy(send, recv, ssem, rsem, d):
+        q = lax.rem(p + d, NP)
+        return remote(send.at[d - 1], recv.at[p], ssem.at[d - 1], rsem.at[p], at_plane(q))
+
+    def spread(weight, send, recv, ssem, rsem, own):
+        @pl.loop(1, NP)
+        def _(d):
+            send[d - 1] = product(lax.rem(p + d, NP), weight).astype(jnp.bfloat16)
+            part_copy(send, recv, ssem, rsem, d).start()
+
+        own[...] = product(p, weight)
+
+    def collect(send, recv, ssem, rsem, own):
+        for d in range(1, NP):
+            q = lax.rem(p + d, NP)
+            remote(send.at[0], recv.at[q], ssem.at[0], rsem.at[q], at_plane(q)).wait_recv()
+            own[...] += recv[q].astype(jnp.float32)
+
+    spread(a_all, pa_send, pa_recv, pa_ssem, pa_rsem, total_a)
+    weight_wait(w_send, w_all, w_ssem, w_rsem)
+    own_w.wait()
     for i in range(1, G):
         o_copy(i).start()
-    own_o = pltpu.make_async_copy(o_send.at[G - 1], o_all.at[j], local_sem.at[2])
-    own_o.start()
-
-    def product(prompt):
-        x = normed[pl.ds(prompt * L, L)].reshape(seq, G * rows)
-        w = w_all[...].reshape(G * rows, width)
-        return jnp.dot(x, w, preferred_element_type=jnp.float32)
-
-    def p_copy(d):
-        q = lax.rem(p + d, NP)
-        return remote(
-            part_send.at[d - 1], part_recv.at[p], p_ssem.at[d - 1], p_rsem.at[p], at_plane(q)
-        )
-
-    @pl.loop(1, NP)
-    def _(d):
-        part_send[d - 1] = product(lax.rem(p + d, NP)).astype(jnp.bfloat16)
-        p_copy(d).start()
-
-    total[...] = product(p)
-    for d in range(1, NP):
-        q = lax.rem(p + d, NP)
-        remote(
-            part_send.at[0], part_recv.at[q], p_ssem.at[0], p_rsem.at[q], at_plane(q)
-        ).wait_recv()
-        total[...] += part_recv[q].astype(jnp.float32)
+    spread(w_all, pb_send, pb_recv, pb_ssem, pb_rsem, total_b)
+    collect(pa_send, pa_recv, pa_ssem, pa_rsem, total_a)
 
     @pl.when(s == p)
     def _():
@@ -474,44 +512,75 @@
             jnp.bfloat16
         )
 
-    key_rows = rotate(total[:, hc : hc + HEAD_DIMENSION])
-    value_rows = total[:, hc + HEAD_DIMENSION :].astype(jnp.bfloat16)
+    raw = total_a[:, first:]
+    keyval[core] = jnp.where(core == 0, rotate(raw), raw.astype(jnp.bfloat16))
+
+    def k_copy(index):
+        return remote(keyval.at[index], keyval.at[index], k_ssem, k_rsem, (sibling, p, l))
+
+    k_copy(core).start()
+
+    def positions(index):
+        place = index
+        for block in range(1, L * NP):
+            here, before = (
+                ((b % NP) * L + b // NP) * tokens - b * tokens for b in (block, block - 1)
+            )
+            place += jnp.where(index >= block * tokens, here - before, 0)
+        return place
+
+    column = positions(lax.broadcasted_iota(jnp.int32, (1, seq), 1))
+    row = positions(lax.broadcasted_iota(jnp.int32, (seq, 1), 0))
     limit = jnp.concatenate([length_here[0:1, :]] * (seq // 128), axis=1)
-    column = columns_at[0:1, :]
-    allowed = (column <= rows_at[...]) & (column < limit)
-    for h in range(hc // HEAD_DIMENSION):
-        at = slice(h * HEAD_DIMENSION, (h + 1) * HEAD_DIMENSION)
-        scores = lax.dot_general(
-            rotate(total[:, at]),
-            key_rows,
-            (((1,), (1,)), ((), ())),
-            preferred_element_type=jnp.float32,
-        ) / math.sqrt(HEAD_DIMENSION)
-        scores = jnp.where(allowed, scores, masked_score)
-        exponent = jnp.exp(scores - jnp.max(scores, axis=-1, keepdims=True))
-        attention = (exponent / jnp.sum(exponent, axis=-1, keepdims=True)).astype(jnp.bfloat16)
-        heads[p, :, at] = jnp.dot(
-            attention, value_rows, preferred_element_type=jnp.float32
-        ).astype(jnp.bfloat16)
-
+    allowed = (column <= row) & (column < limit)
+    k_copy(1 - core).wait_recv()
+
+    def attend(own, n_columns, gathered):
+        for h in range(n_columns // HEAD_DIMENSION):
+            at = slice(h * HEAD_DIMENSION, (h + 1) * HEAD_DIMENSION)
+            scores = lax.dot_general(
+                rotate(own[:, at]),
+                keyval[0],
+                (((1,), (1,)), ((), ())),
+                preferred_element_type=jnp.float32,
+            ) / math.sqrt(HEAD_DIMENSION)
+            scores = jnp.where(allowed, scores, masked_score)
+            exponent = jnp.exp(scores - jnp.max(scores, axis=-1, keepdims=True))
+            attention = exponent / jnp.sum(exponent, axis=-1, keepdims=True)
+            gathered[p, :, at] = jnp.dot(
+                attention.astype(jnp.bfloat16), keyval[1], preferred_element_type=jnp.float32
+            ).astype(jnp.bfloat16)
+
+    def head_copy(gathered, ssem, rsem, d):
+        return remote(
+            gathered.at[p], gathered.at[p], ssem.at[d], rsem.at[p], at_plane(lax.rem(p + d, NP))
+        )
+
+    attend(total_a, first, heads_a)
     for d in range(1, NP):
-        remote(
-            heads.at[p], heads.at[p], h_ssem.at[d], h_rsem.at[p], at_plane(lax.rem(p + d, NP))
-        ).start()
-
-    for d in range(1, G):
-        src = lax.rem(j + d, G)
-        remote(o_send.at[0], o_all.at[src], o_ssem.at[0], o_rsem.at[src], member(src)).wait_recv()
+        head_copy(heads_a, ha_ssem, ha_rsem, d).start()
+    collect(pb_send, pb_recv, pb_ssem, pb_rsem, total_b)
+    attend(total_b, split, heads_b)
+    for d in range(1, NP):
+        head_copy(heads_b, hb_ssem, hb_rsem, d).start()
+
+    weight_wait(o_send, o_all, o_ssem, o_rsem)
     own_o.wait()
 
     def heads_wait(q):
         @pl.when(q != p)
         def _():
-            remote(heads.at[q], heads.at[q], h_ssem.at[0], h_rsem.at[q], at_plane(q)).wait_recv()
+            for gathered, ssem, rsem in ((heads_a, ha_ssem, ha_rsem), (heads_b, hb_ssem, hb_rsem)):
+                remote(
+                    gathered.at[q], gathered.at[q], ssem.at[0], rsem.at[q], at_plane(q)
+                ).wait_recv()
 
     def features(prompt, b):
+        over = (((1,), (1,)), ((), ()))
         return lax.dot_general(
-            heads[prompt], o_all[b], (((1,), (1,)), ((), ())), preferred_element_type=jnp.float32
+            heads_a[prompt], o_all[b, :, 0:first], over, preferred_element_type=jnp.float32
+        ) + lax.dot_general(
+            heads_b[prompt], o_all[b, :, first:], over, preferred_element_type=jnp.float32
         )
 
     def b_copy(e):
@@ -519,46 +588,54 @@
             pair_send.at[e], pair_recv.at[e], b_ssem.at[e], b_rsem.at[e], (sibling, p, l)
         )
 
+    here = pair * L + l
+
+    def r_copy(e, dl, start):
+        chip = lax.rem(p // 2 + e, half)
+        lane = lax.rem(l + dl, L)
+
+        @pl.when((chip * L + lane) != here)
+        def _():
+            copy = remote(
+                red_send.at[e, lane],
+                red_recv.at[here],
+                r_ssem.at[e, dl],
+                r_rsem.at[here],
+                (2 * chip + core, p, lane),
+            )
+            if start:
+                copy.start()
+            else:
+                copy.wait_send()
+
     for e in range(half):
-        prompt = 2 * lax.rem(pair + e, half) + 1 - core
-        heads_wait(prompt)
+        theirs = 2 * lax.rem(p // 2 + e, half) + 1 - core
+        mine = 2 * lax.rem(p // 2 + e, half) + core
+        heads_wait(theirs)
 
         @pl.loop(0, G)
         def _(b):
             at = pl.ds(pl.multiple_of(b * rows, 128), rows)
-            pair_send[e, :, at] = features(prompt, b).astype(jnp.bfloat16)
+            pair_send[e, :, at] = features(theirs, b).astype(jnp.bfloat16)
 
         b_copy(e).start()
-
-    here = pair * L + l
-
-    def r_copy(da, dl, n):
-        sec, lane = same_core[da * L + dl]
-        return remote(
-            red_send.at[da, lane], red_recv.at[here], r_ssem.at[n], r_rsem.at[here], (sec, p, lane)
-        )
-
-    for e in list(range(1, half)) + [0]:
-        prompt = 2 * lax.rem(pair + e, half) + core
-        heads_wait(prompt)
+        heads_wait(mine)
         b_copy(e).wait_recv()
 
         @pl.loop(0, G)
         def _(b):
             at = pl.ds(pl.multiple_of(b * rows, 128), rows)
-            value = features(prompt, b) + pair_recv[e, :, at].astype(jnp.float32)
+            value = features(mine, b) + pair_recv[e, :, at].astype(jnp.float32)
             red_send[e, :, :, at] = value.astype(jnp.bfloat16).reshape(L, seq // L, rows)
 
         for dl in range(L):
-            if e or dl:
-                r_copy(e, dl, e * L + dl).start()
-
-    summed = red_send[0, l].astype(jnp.float32)
-    for n in range(1, half * L):
-        sec, lane = same_core[n]
+            r_copy(e, dl, True)
+
+    summed = red_send[lax.rem(pair + half - p // 2, half), l].astype(jnp.float32)
+    for sec, lane in others:
         src = (sec // 2) * L + lane
         remote(
-            red_send.at[0, l], red_recv.at[src], r_ssem.at[0], r_rsem.at[src], (sec, p, lane)
+            red_send.at[0, l], red_recv.at[src], r_ssem.at[0, 0], r_rsem.at[src], (sec, p, lane)
         ).wait_recv()
         summed += red_recv[src].astype(jnp.float32)
     z_send[...] = summed.astype(jnp.bfloat16).reshape(NP, tokens, G * rows)
@@ -580,20 +657,24 @@
     for d in range(1, NP):
         q = lax.rem(p + d, NP)
         x_copy(q, p, d).wait_send()
-        p_copy(d).wait_send()
-        remote(heads.at[p], heads.at[p], h_ssem.at[d], h_rsem.at[p], at_plane(q)).wait_send()
+        part_copy(pa_send, pa_recv, pa_ssem, pa_rsem, d).wait_send()
+        part_copy(pb_send, pb_recv, pb_ssem, pb_rsem, d).wait_send()
+        head_copy(heads_a, ha_ssem, ha_rsem, d).wait_send()
+        head_copy(heads_b, hb_ssem, hb_rsem, d).wait_send()
         z_copy(q, d).wait_send()
     for i in range(1, G):
+        a_copy(i).wait_send()
         w_copy(i).wait_send()
         o_copy(i).wait_send()
     for n, (sec, lane) in enumerate(others):
         g_copy(j, g_ssem.at[n], (sec, p, lane)).wait_send()
     for n, (sec, lane) in enumerate(same_core):
         g_copy(sec * L + lane, f_ssem.at[n], (sibling, p, l)).wait_send()
+    k_copy(core).wait_send()
     for e in range(half):
         b_copy(e).wait_send()
-    for n in range(1, half * L):
-        r_copy(n // L, n % L, n).wait_send()
+        for dl in range(L):
+            r_copy(e, dl, False)
 
 
 def fused(hidden, norm_gain, lengths, *weights):
@@ -602,30 +683,37 @@
     half = S // 2
     rows = weights[0].shape[0]
     hc = weights[0].shape[1] // G
-    width = hc + 2 * HEAD_DIMENSION
+    first = hc // 2
+    split = hc - first
+    width = first + HEAD_DIMENSION
     tokens = hidden.shape[1]
     seq = tokens * NP * L
     order = np.arange(seq).reshape(NP, L, tokens).transpose(1, 0, 2).reshape(seq)
     cosine, sine = rope_tables(order)
-    rows_at = np.broadcast_to(order.astype(np.int32)[:, None], (seq, seq))
-    columns_at = np.broadcast_to(order.astype(np.int32)[None, :], (8, seq))
-    length = jnp.broadcast_to(lengths[:, None], (8, 128))
     bf, f32 = jnp.bfloat16, jnp.float32
     dma = pltpu.SemaphoreType.DMA
     vmem = pl.BlockSpec(memory_space=pltpu.VMEM)
     hbm = pl.BlockSpec(memory_space=pl.ANY)
+    smem = pl.BlockSpec(memory_space=pltpu.SMEM)
     scratch = [
-        pltpu.VMEM((2, 4, rows, width), f32),
+        pltpu.VMEM((2, 4, rows, max(width, hc)), f32),
         pltpu.VMEM((G, rows, width), bf),
         pltpu.VMEM((G, rows, width), bf),
+        pltpu.VMEM((G, rows, split), bf),
+        pltpu.VMEM((G, rows, split), bf),
         pltpu.VMEM((G, rows, hc), bf),
         pltpu.VMEM((G, rows, hc), bf),
         pltpu.VMEM((NP, tokens, G * rows), bf),
         pltpu.VMEM((G, NP, tokens, G * rows), bf),
         pltpu.VMEM((NP - 1, seq, width), bf),
         pltpu.VMEM((NP, seq, width), bf),
+        pltpu.VMEM((NP - 1, seq, split), bf),
+        pltpu.VMEM((NP, seq, split), bf),
         pltpu.VMEM((seq, width), f32),
-        pltpu.VMEM((NP, seq, hc), bf),
+        pltpu.VMEM((seq, split), f32),
+        pltpu.VMEM((2, seq, HEAD_DIMENSION), bf),
+        pltpu.VMEM((NP, seq, first), bf),
+        pltpu.VMEM((NP, seq, split), bf),
         pltpu.VMEM((half, seq, G * rows), bf),
         pltpu.VMEM((half, seq, G * rows), bf),
         pltpu.VMEM((half, L, seq // L, G * rows), bf),
@@ -633,34 +721,24 @@
         pltpu.VMEM((NP, tokens, G * rows), bf),
         pltpu.VMEM((NP, tokens, G * rows), bf),
         pltpu.VMEM((8, 128), jnp.int32),
-        dma((2, 4, 3)),
-        dma((3,)),
-        dma((G,)),
-        dma((G,)),
-        dma((G,)),
-        dma((G,)),
-        dma((NP,)),
-        dma((NP,)),
-        dma((half * L,)),
-        dma((G,)),
-        dma((half * L,)),
-        dma((NP,)),
-        dma((NP,)),
-        dma((NP,)),
-        dma((NP,)),
-        dma((half,)),
-        dma((half,)),
-        dma((half * L,)),
-        dma((half * L,)),
-        dma((NP,)),
-        dma((NP,)),
-        dma((S,)),
-        dma,
+        pltpu.VMEM((8, 128), jnp.int32),
+        dma((2, 4, 2)),
+        dma((4,)),
     ]
+    scratch += [dma((G,))] * 6
+    scratch += [dma((NP,))] * 2
+    scratch += [dma((half * L,)), dma((G,)), dma((half * L,))]
+    scratch += [dma((NP,))] * 4
+    scratch += [dma, dma]
+    scratch += [dma((NP,))] * 4
+    scratch += [dma((half,))] * 2
+    scratch += [dma((half, L)), dma((half * L,))]
+    scratch += [dma((NP,))] * 2
+    scratch += [dma((S,)), dma]
     result = pl.pallas_call(
         functools.partial(block_kernel, (S, NP, L)),
         out_shape=jax.ShapeDtypeStruct(hidden.shape[1:], bf),
-        in_specs=[vmem] * 7 + [hbm] * 12,
+        in_specs=[vmem, vmem, smem, vmem, vmem] + [hbm] * 12,
         out_specs=vmem,
         scratch_shapes=scratch,
         compiler_params=pltpu.CompilerParams(
@@ -672,11 +750,9 @@
     )(
         hidden[0],
         norm_gain[None, :],
-        length,
+        lengths,
         jnp.asarray(cosine),
         jnp.asarray(sine),
-        jnp.asarray(rows_at),
-        jnp.asarray(columns_at),
         *weights,
     )
     return result[None]
@@ -687,6 +763,8 @@
         hidden.shape[1] % 16 == 0
         and weights[0].shape[0] % 128 == 0
         and lax.axis_size("section") % 2 == 0
+        and lax.axis_size("section") * lax.axis_size("lane") == 2 * KEYVAL_HEADS
+        and weights[0].shape[1] % (4 * HEAD_DIMENSION * KEYVAL_HEADS) == 0
     )
     return (fused if whole_tiles else on_device)(hidden, norm_gain, lengths, *weights)
 

time: 179 us -> 149 us (0.83)
  the two profiles are of different devices: /device:TPU:17 before, /device:TPU:0 now
where the time goes in v3:
time: 149 us
  Pallas kernels  146 us (98%)
  local copies, waits for them, and re-layouts  1.87 us (1%)
    pallas_call x1, Pallas kernels, fused(): pl.pallas_call(functools.partial(block_kernel, (S, NP, L)), out_shape=jax...  146 us

profile of v3, /device:TPU:0, one launch (start us, length us, event | category | flops | bytes accessed | tf_op | source)
XLA Modules:
  0.0 148.7 jit_solution(13618835141823340114)
XLA Ops:
  0.7 146.1 %shard_map.163 = bf16[32,8192]{1,0:T(8,128)(2,1)} custom-call(bf16[32,8192]{1,0:T(8,128)(2,1)} %bitcast.4, f32[1,8192]{1,0:T(1,128)} %bitcast.5, s32[1]{0:T(128)S(6)} %copy.19.lengths, f32[256,128]{1,0:T(8,128)} %constant.4.clone.cosine, f32[256,128]{1,0:T(8,128)} %constant.5.clone.sine, f32[256,4096]{1,0:T(8,128)} %qp.1, f32[256,4096]{1,0:T(8,128)} %qg.1, ...), custom_call_target="tpu_custom_call" | custom-call | flops 8000000000 | bytes 40000000 | tf_op jit(solution)/shard_map/pallas_call | solution.py:738
  146.8 1.9 %copy.20 = bf16[1,32,8192]{2,1,0:T(8,128)(2,1)} copy(bf16[1,32,8192]{2,1,0:T(8,128)(2,1)} %bitcast.3) | data formatting | bytes 1048576

commit v4 on v3

--- a/solution.py
+++ b/solution.py
@@ -284,6 +284,12 @@
             device_id_type=pl.DeviceIdType.MESH,
         )
 
+    def section_of(plane):
+        core_of = lax.rem(plane, 2)
+        return 2 * lax.rem(plane // 2 + core_of, half) + core_of
+
+    kept = section_of(p)
+
     same_core = []
     for da in range(half):
         for dl in range(L):
@@ -378,7 +384,7 @@
 
     pl.semaphore_wait(barrier, G - 1 + NP - 1)
 
-    @pl.when(s == p)
+    @pl.when(s == kept)
     def _():
         for d in range(1, S):
             remote(
@@ -464,8 +470,8 @@
         block = (sec + 1 - 2 * core) * L + lane
         g_copy(block, f_ssem.at[n], (sibling, p, l)).wait_recv()
 
-    def product(prompt, weight):
-        x = normed[pl.ds(prompt * L, L)].reshape(seq, G * rows)
+    def product(plane, weight):
+        x = normed[pl.ds(section_of(plane) * L, L)].reshape(seq, G * rows)
         w = weight[...].reshape(G * rows, weight.shape[2])
         return jnp.dot(x, w, preferred_element_type=jnp.float32)
 
@@ -495,7 +501,7 @@
     spread(w_all, pb_send, pb_recv, pb_ssem, pb_rsem, total_b)
     collect(pa_send, pa_recv, pa_ssem, pa_rsem, total_a)
 
-    @pl.when(s == p)
+    @pl.when(s == kept)
     def _():
         length_here[...] = length[...]
         for d in range(1, S):
@@ -503,9 +509,9 @@
                 length, length_here, l_ssem.at[d], l_rsem, (lax.rem(s + d, S), p, l)
             ).wait_send()
 
-    @pl.when(s != p)
+    @pl.when(s != kept)
     def _():
-        remote(length, length_here, l_ssem.at[0], l_rsem, (p, p, l)).wait_recv()
+        remote(length, length_here, l_ssem.at[0], l_rsem, (kept, p, l)).wait_recv()
 
     def rotate(x):
         return (x * cosine[...] + pltpu.roll(x, HEAD_DIMENSION // 2, 1) * sine[...]).astype(
@@ -591,7 +597,7 @@
     here = pair * L + l
 
     def r_copy(e, dl, start):
-        chip = lax.rem(p // 2 + e, half)
+        chip = lax.rem(p // 2 + e + core, half)
         lane = lax.rem(l + dl, L)
 
         @pl.when((chip * L + lane) != here)
@@ -631,7 +637,7 @@
         for dl in range(L):
             r_copy(e, dl, True)
 
-    summed = red_send[lax.rem(pair + half - p // 2, half), l].astype(jnp.float32)
+    summed = red_send[lax.rem(pair + 2 * half - core - p // 2, half), l].astype(jnp.float32)
     for sec, lane in others:
         src = (sec // 2) * L + lane
         remote(

time: 149 us -> 148 us (level)
  Pallas kernels: 146 us -> 144 us
    pallas_call x1, Pallas kernels: 146 us -> 144 us  [fused(): pl.pallas_call(functools.partial(block_kernel, (S, NP, L)), out_shape=jax...]
where the time goes in v4:
time: 148 us; the launch traced here: 147 us
  Pallas kernels  144 us (97%)
  local copies, waits for them, and re-layouts  1.87 us (1%)
    pallas_call x1, Pallas kernels, fused(): pl.pallas_call(functools.partial(block_kernel, (S, NP, L)), out_shape=jax...  144 us

profile of v4, /device:TPU:0, one launch (start us, length us, event | category | flops | bytes accessed | tf_op | source)
XLA Modules:
  0.0 146.8 jit_solution(2403895696680249392)
XLA Ops:
  0.7 144.3 %shard_map.163 = bf16[32,8192]{1,0:T(8,128)(2,1)} custom-call(bf16[32,8192]{1,0:T(8,128)(2,1)} %bitcast.4, f32[1,8192]{1,0:T(1,128)} %bitcast.5, s32[1]{0:T(128)S(6)} %copy.19.lengths, f32[256,128]{1,0:T(8,128)} %constant.4.clone.cosine, f32[256,128]{1,0:T(8,128)} %constant.5.clone.sine, f32[256,4096]{1,0:T(8,128)} %qp.1, f32[256,4096]{1,0:T(8,128)} %qg.1, ...), custom_call_target="tpu_custom_call" | custom-call | flops 8000000000 | bytes 40000000 | tf_op jit(solution)/shard_map/pallas_call | solution.py:744
  144.9 1.9 %copy.20 = bf16[1,32,8192]{2,1,0:T(8,128)(2,1)} copy(bf16[1,32,8192]{2,1,0:T(8,128)(2,1)} %bitcast.3) | data formatting | bytes 1048576

commit v5 on v4

--- a/solution.py
+++ b/solution.py
@@ -232,6 +232,8 @@
     x_rsem,
     g_ssem,
     g_rsem,
+    d_ssem,
+    d_rsem,
     f_ssem,
     pa_ssem,
     pa_rsem,
@@ -450,20 +452,32 @@
     def g_copy(block, ssem, device):
         return remote(normed.at[block], normed.at[block], ssem, g_rsem.at[block], device)
 
-    for n, (sec, lane) in enumerate(others):
-        g_copy(j, g_ssem.at[n], (sec, p, lane)).start()
+    by_lane, by_section, corner = others
+    lane_block, section_block, corner_block = (sec * L + lane for sec, lane in others)
+    to_lane, to_section = ((sec, p, lane) for sec, lane in (by_lane, by_section))
+    g_copy(j, g_ssem.at[0], to_lane).start()
+    g_copy(j, g_ssem.at[1], to_section).start()
     g_copy(j, f_ssem.at[0], (sibling, p, l)).start()
+
+    def corner_copy(block, part, device):
+        view = normed.at[block, pl.ds(part * (NP // 2), NP // 2)]
+        return remote(view, view, d_ssem.at[part], d_rsem.at[part], device)
 
     update_all(job_o, None, hc, o_send, lambda i: None)
     own_o = pltpu.make_async_copy(o_send.at[G - 1], o_all.at[j], local_sem.at[3])
     own_o.start()
 
-    for n, (sec, lane) in enumerate(others):
-        block = sec * L + lane
-        g_copy(block, g_ssem.at[n], (sec, p, lane)).wait_recv()
-        g_copy(block, f_ssem.at[n + 1], (sibling, p, l)).start()
+    g_copy(section_block, g_ssem.at[1], to_section).wait_recv()
+    corner_copy(section_block, 0, to_lane).start()
+    g_copy(section_block, f_ssem.at[2], (sibling, p, l)).start()
+    g_copy(lane_block, g_ssem.at[0], to_lane).wait_recv()
+    corner_copy(lane_block, 1, to_section).start()
+    g_copy(lane_block, f_ssem.at[1], (sibling, p, l)).start()
     for i in range(1, G):
         w_copy(i).start()
+    corner_copy(corner_block, 0, to_lane).wait_recv()
+    corner_copy(corner_block, 1, to_section).wait_recv()
+    g_copy(corner_block, f_ssem.at[3], (sibling, p, l)).start()
     weight_wait(a_send, a_all, a_ssem, a_rsem)
     own_a.wait()
     for n, (sec, lane) in enumerate(same_core):
@@ -589,24 +603,28 @@
             heads_b[prompt], o_all[b, :, first:], over, preferred_element_type=jnp.float32
         )
 
-    def b_copy(e):
+    def b_copy(e, part):
         return remote(
-            pair_send.at[e], pair_recv.at[e], b_ssem.at[e], b_rsem.at[e], (sibling, p, l)
+            pair_send.at[e, part],
+            pair_recv.at[e, part],
+            b_ssem.at[e, part],
+            b_rsem.at[e, part],
+            (sibling, p, l),
         )
 
     here = pair * L + l
 
-    def r_copy(e, dl, start):
+    def r_copy(e, part, dl, start):
         chip = lax.rem(p // 2 + e + core, half)
         lane = lax.rem(l + dl, L)
 
         @pl.when((chip * L + lane) != here)
         def _():
             copy = remote(
-                red_send.at[e, lane],
-                red_recv.at[here],
-                r_ssem.at[e, dl],
-                r_rsem.at[here],
+                red_send.at[e, part, lane],
+                red_recv.at[here, part],
+                r_ssem.at[e, part, dl],
+                r_rsem.at[here, part],
                 (2 * chip + core, p, lane),
             )
             if start:
@@ -618,47 +636,72 @@
         theirs = 2 * lax.rem(p // 2 + e, half) + 1 - core
         mine = 2 * lax.rem(p // 2 + e, half) + core
         heads_wait(theirs)
-
-        @pl.loop(0, G)
-        def _(b):
-            at = pl.ds(pl.multiple_of(b * rows, 128), rows)
-            pair_send[e, :, at] = features(theirs, b).astype(jnp.bfloat16)
-
-        b_copy(e).start()
+        for part in range(2):
+
+            @pl.loop(0, G // 2)
+            def _(b):
+                at = pl.ds(pl.multiple_of(b * rows, 128), rows)
+                value = features(theirs, part * (G // 2) + b)
+                pair_send[e, part, :, at] = value.astype(jnp.bfloat16)
+
+            b_copy(e, part).start()
         heads_wait(mine)
-        b_copy(e).wait_recv()
-
-        @pl.loop(0, G)
-        def _(b):
-            at = pl.ds(pl.multiple_of(b * rows, 128), rows)
-            value = features(mine, b) + pair_recv[e, :, at].astype(jnp.float32)
-            red_send[e, :, :, at] = value.astype(jnp.bfloat16).reshape(L, seq // L, rows)
-
-        for dl in range(L):
-            r_copy(e, dl, True)
-
-    summed = red_send[lax.rem(pair + 2 * half - core - p // 2, half), l].astype(jnp.float32)
-    for sec, lane in others:
-        src = (sec // 2) * L + lane
-        remote(
-            red_send.at[0, l], red_recv.at[src], r_ssem.at[0, 0], r_rsem.at[src], (sec, p, lane)
-        ).wait_recv()
-        summed += red_recv[src].astype(jnp.float32)
-    z_send[...] = summed.astype(jnp.bfloat16).reshape(NP, tokens, G * rows)
-
-    def z_copy(q, d):
-        return remote(z_send.at[q], z_recv.at[p], z_ssem.at[d], z_rsem.at[p], at_plane(q))
-
-    for d in range(1, NP):
-        z_copy(lax.rem(p + d, NP), d).start()
-    z_recv[p] = z_send[p]
-    for d in range(1, NP):
-        q = lax.rem(p + d, NP)
-        remote(z_send.at[q], z_recv.at[q], z_ssem.at[d], z_rsem.at[q], at_plane(q)).wait_recv()
+        for part in range(2):
+            b_copy(e, part).wait_recv()
+
+            @pl.loop(0, G // 2)
+            def _(b):
+                at = pl.ds(pl.multiple_of(b * rows, 128), rows)
+                value = features(mine, part * (G // 2) + b)
+                value += pair_recv[e, part, :, at].astype(jnp.float32)
+                red_send[e, part, :, :, at] = value.astype(jnp.bfloat16).reshape(
+                    L, seq // L, rows
+                )
+
+            for dl in range(L):
+                r_copy(e, part, dl, True)
+
+    def z_copy(q, part, d):
+        return remote(
+            z_send.at[part, q],
+            z_recv.at[part, p],
+            z_ssem.at[part, d],
+            z_rsem.at[part, p],
+            at_plane(q),
+        )
+
+    for part in range(2):
+        summed = red_send[lax.rem(pair + 2 * half - core - p // 2, half), part, l].astype(
+            jnp.float32
+        )
+        for sec, lane in others:
+            src = (sec // 2) * L + lane
+            remote(
+                red_send.at[0, part, l],
+                red_recv.at[src, part],
+                r_ssem.at[0, part, 0],
+                r_rsem.at[src, part],
+                (sec, p, lane),
+            ).wait_recv()
+            summed += red_recv[src, part].astype(jnp.float32)
+        z_send[part] = summed.astype(jnp.bfloat16).reshape(NP, tokens, G * rows // 2)
+        for d in range(1, NP):
+            z_copy(lax.rem(p + d, NP), part, d).start()
+        z_recv[part, p] = z_send[part, p]
+    for part in range(2):
+        for d in range(1, NP):
+            q = lax.rem(p + d, NP)
+            remote(
+                z_send.at[part, q],
+                z_recv.at[part, q],
+                z_ssem.at[part, d],
+                z_rsem.at[part, q],
+                at_plane(q),
+            ).wait_recv()
     for c in range(S * NP):
-        out[:, c * strip : (c + 1) * strip] = z_recv[
-            c % NP, :, (c // NP) * strip : (c // NP + 1) * strip
-        ]
+        sec = c // NP
+        at = (sec % half) * strip
+        out[:, c * strip : (c + 1) * strip] = z_recv[sec // half, c % NP, :, at : at + strip]
 
     for d in range(1, NP):
         q = lax.rem(p + d, NP)
@@ -667,20 +710,24 @@
         part_copy(pb_send, pb_recv, pb_ssem, pb_rsem, d).wait_send()
         head_copy(heads_a, ha_ssem, ha_rsem, d).wait_send()
         head_copy(heads_b, hb_ssem, hb_rsem, d).wait_send()
-        z_copy(q, d).wait_send()
+        for part in range(2):
+            z_copy(q, part, d).wait_send()
     for i in range(1, G):
         a_copy(i).wait_send()
         w_copy(i).wait_send()
         o_copy(i).wait_send()
-    for n, (sec, lane) in enumerate(others):
-        g_copy(j, g_ssem.at[n], (sec, p, lane)).wait_send()
+    g_copy(j, g_ssem.at[0], to_lane).wait_send()
+    g_copy(j, g_ssem.at[1], to_section).wait_send()
+    corner_copy(section_block, 0, to_lane).wait_send()
+    corner_copy(lane_block, 1, to_section).wait_send()
     for n, (sec, lane) in enumerate(same_core):
         g_copy(sec * L + lane, f_ssem.at[n], (sibling, p, l)).wait_send()
     k_copy(core).wait_send()
     for e in range(half):
-        b_copy(e).wait_send()
-        for dl in range(L):
-            r_copy(e, dl, False)
+        for part in range(2):
+            b_copy(e, part).wait_send()
+            for dl in range(L):
+                r_copy(e, part, dl, False)
 
 
 def fused(hidden, norm_gain, lengths, *weights):
@@ -720,12 +767,12 @@
         pltpu.VMEM((2, seq, HEAD_DIMENSION), bf),
         pltpu.VMEM((NP, seq, first), bf),
         pltpu.VMEM((NP, seq, split), bf),
-        pltpu.VMEM((half, seq, G * rows), bf),
-        pltpu.VMEM((half, seq, G * rows), bf),
-        pltpu.VMEM((half, L, seq // L, G * rows), bf),
-        pltpu.VMEM((half * L, seq // L, G * rows), bf),
-        pltpu.VMEM((NP, tokens, G * rows), bf),
-        pltpu.VMEM((NP, tokens, G * rows), bf),
+        pltpu.VMEM((half, 2, seq, G * rows // 2), bf),
+        pltpu.VMEM((half, 2, seq, G * rows // 2), bf),
+        pltpu.VMEM((half, 2, L, seq // L, G * rows // 2), bf),
+        pltpu.VMEM((half * L, 2, seq // L, G * rows // 2), bf),
+        pltpu.VMEM((2, NP, tokens, G * rows // 2), bf),
+        pltpu.VMEM((2, NP, tokens, G * rows // 2), bf),
         pltpu.VMEM((8, 128), jnp.int32),
         pltpu.VMEM((8, 128), jnp.int32),
         dma((2, 4, 2)),
@@ -733,13 +780,13 @@
     ]
     scratch += [dma((G,))] * 6
     scratch += [dma((NP,))] * 2
-    scratch += [dma((half * L,)), dma((G,)), dma((half * L,))]
+    scratch += [dma((half * L,)), dma((G,)), dma((2,)), dma((2,)), dma((half * L,))]
     scratch += [dma((NP,))] * 4
     scratch += [dma, dma]
     scratch += [dma((NP,))] * 4
-    scratch += [dma((half,))] * 2
-    scratch += [dma((half, L)), dma((half * L,))]
-    scratch += [dma((NP,))] * 2
+    scratch += [dma((half, 2))] * 2
+    scratch += [dma((half, 2, L)), dma((half * L, 2))]
+    scratch += [dma((2, NP))] * 2
     scratch += [dma((S,)), dma]
     result = pl.pallas_call(
         functools.partial(block_kernel, (S, NP, L)),
@@ -770,6 +817,8 @@
         and weights[0].shape[0] % 128 == 0
         and lax.axis_size("section") % 2 == 0
         and lax.axis_size("section") * lax.axis_size("lane") == 2 * KEYVAL_HEADS
+        and lax.axis_size("section") == 2 * lax.axis_size("lane")
+        and lax.axis_size("plane") % 2 == 0
         and weights[0].shape[1] % (4 * HEAD_DIMENSION * KEYVAL_HEADS) == 0
     )
     return (fused if whole_tiles else on_device)(hidden, norm_gain, lengths, *weights)

time: 148 us -> 134 us (0.905)
  Pallas kernels: 144 us -> 131 us
    pallas_call x1, Pallas kernels: 144 us -> 131 us  [fused(): pl.pallas_call(functools.partial(block_kernel, (S, NP, L)), out_shape=jax...]
where the time goes in v5:
time: 134 us; the launch traced here: 133 us
  Pallas kernels  131 us (98%)
  local copies, waits for them, and re-layouts  1.87 us (1%)
    pallas_call x1, Pallas kernels, fused(): pl.pallas_call(functools.partial(block_kernel, (S, NP, L)), out_shape=jax...  131 us

profile of v5, /device:TPU:0, one launch (start us, length us, event | category | flops | bytes accessed | tf_op | source)
XLA Modules:
  0.0 133.5 jit_solution(13687579170418891932)
XLA Ops:
  0.7 131.0 %shard_map.163 = bf16[32,8192]{1,0:T(8,128)(2,1)} custom-call(bf16[32,8192]{1,0:T(8,128)(2,1)} %bitcast.4, f32[1,8192]{1,0:T(1,128)} %bitcast.5, s32[1]{0:T(128)S(6)} %copy.19.lengths, f32[256,128]{1,0:T(8,128)} %constant.4.clone.cosine, f32[256,128]{1,0:T(8,128)} %constant.5.clone.sine, f32[256,4096]{1,0:T(8,128)} %qp.1, f32[256,4096]{1,0:T(8,128)} %qg.1, ...), custom_call_target="tpu_custom_call" | custom-call | flops 8000000000 | bytes 40000000 | tf_op jit(solution)/shard_map/pallas_call | solution.py:791
  131.6 1.9 %copy.20 = bf16[1,32,8192]{2,1,0:T(8,128)(2,1)} copy(bf16[1,32,8192]{2,1,0:T(8,128)(2,1)} %bitcast.3) | data formatting | bytes 1048576

commit v6 on v5

--- a/solution.py
+++ b/solution.py
@@ -268,6 +268,7 @@
     hc = first + split
     tokens = hidden.shape[0]
     strip = L * rows
+    parts = S
     seq = NP * tokens * L
 
     def member(m):
@@ -636,23 +637,23 @@
         theirs = 2 * lax.rem(p // 2 + e, half) + 1 - core
         mine = 2 * lax.rem(p // 2 + e, half) + core
         heads_wait(theirs)
-        for part in range(2):
-
-            @pl.loop(0, G // 2)
+        for part in range(parts):
+
+            @pl.loop(0, G // parts)
             def _(b):
                 at = pl.ds(pl.multiple_of(b * rows, 128), rows)
-                value = features(theirs, part * (G // 2) + b)
+                value = features(theirs, part * (G // parts) + b)
                 pair_send[e, part, :, at] = value.astype(jnp.bfloat16)
 
             b_copy(e, part).start()
         heads_wait(mine)
-        for part in range(2):
+        for part in range(parts):
             b_copy(e, part).wait_recv()
 
-            @pl.loop(0, G // 2)
+            @pl.loop(0, G // parts)
             def _(b):
                 at = pl.ds(pl.multiple_of(b * rows, 128), rows)
-                value = features(mine, part * (G // 2) + b)
+                value = features(mine, part * (G // parts) + b)
                 value += pair_recv[e, part, :, at].astype(jnp.float32)
                 red_send[e, part, :, :, at] = value.astype(jnp.bfloat16).reshape(
                     L, seq // L, rows
@@ -670,7 +671,7 @@
             at_plane(q),
         )
 
-    for part in range(2):
+    for part in range(parts):
         summed = red_send[lax.rem(pair + 2 * half - core - p // 2, half), part, l].astype(
             jnp.float32
         )
@@ -684,11 +685,11 @@
                 (sec, p, lane),
             ).wait_recv()
             summed += red_recv[src, part].astype(jnp.float32)
-        z_send[part] = summed.astype(jnp.bfloat16).reshape(NP, tokens, G * rows // 2)
+        z_send[part] = summed.astype(jnp.bfloat16).reshape(NP, tokens, G * rows // parts)
         for d in range(1, NP):
             z_copy(lax.rem(p + d, NP), part, d).start()
         z_recv[part, p] = z_send[part, p]
-    for part in range(2):
+    for part in range(parts):
         for d in range(1, NP):
             q = lax.rem(p + d, NP)
             remote(
@@ -699,9 +700,7 @@
                 at_plane(q),
             ).wait_recv()
     for c in range(S * NP):
-        sec = c // NP
-        at = (sec % half) * strip
-        out[:, c * strip : (c + 1) * strip] = z_recv[sec // half, c % NP, :, at : at + strip]
+        out[:, c * strip : (c + 1) * strip] = z_recv[c // NP, c % NP]
 
     for d in range(1, NP):
         q = lax.rem(p + d, NP)
@@ -710,7 +709,7 @@
         part_copy(pb_send, pb_recv, pb_ssem, pb_rsem, d).wait_send()
         head_copy(heads_a, ha_ssem, ha_rsem, d).wait_send()
         head_copy(heads_b, hb_ssem, hb_rsem, d).wait_send()
-        for part in range(2):
+        for part in range(parts):
             z_copy(q, part, d).wait_send()
     for i in range(1, G):
         a_copy(i).wait_send()
@@ -724,7 +723,7 @@
         g_copy(sec * L + lane, f_ssem.at[n], (sibling, p, l)).wait_send()
     k_copy(core).wait_send()
     for e in range(half):
-        for part in range(2):
+        for part in range(parts):
             b_copy(e, part).wait_send()
             for dl in range(L):
                 r_copy(e, part, dl, False)
@@ -767,12 +766,12 @@
         pltpu.VMEM((2, seq, HEAD_DIMENSION), bf),
         pltpu.VMEM((NP, seq, first), bf),
         pltpu.VMEM((NP, seq, split), bf),
-        pltpu.VMEM((half, 2, seq, G * rows // 2), bf),
-        pltpu.VMEM((half, 2, seq, G * rows // 2), bf),
-        pltpu.VMEM((half, 2, L, seq // L, G * rows // 2), bf),
-        pltpu.VMEM((half * L, 2, seq // L, G * rows // 2), bf),
-        pltpu.VMEM((2, NP, tokens, G * rows // 2), bf),
-        pltpu.VMEM((2, NP, tokens, G * rows // 2), bf),
+        pltpu.VMEM((half, S, seq, L * rows), bf),
+        pltpu.VMEM((half, S, seq, L * rows), bf),
+        pltpu.VMEM((half, S, L, seq // L, L * rows), bf),
+        pltpu.VMEM((half * L, S, seq // L, L * rows), bf),
+        pltpu.VMEM((S, NP, tokens, L * rows), bf),
+        pltpu.VMEM((S, NP, tokens, L * rows), bf),
         pltpu.VMEM((8, 128), jnp.int32),
         pltpu.VMEM((8, 128), jnp.int32),
         dma((2, 4, 2)),
@@ -784,9 +783,9 @@
     scratch += [dma((NP,))] * 4
     scratch += [dma, dma]
     scratch += [dma((NP,))] * 4
-    scratch += [dma((half, 2))] * 2
-    scratch += [dma((half, 2, L)), dma((half * L, 2))]
-    scratch += [dma((2, NP))] * 2
+    scratch += [dma((half, S))] * 2
+    scratch += [dma((half, S, L)), dma((half * L, S))]
+    scratch += [dma((S, NP))] * 2
     scratch += [dma((S,)), dma]
     result = pl.pallas_call(
         functools.partial(block_kernel, (S, NP, L)),

time: 134 us -> 134 us (level)
  no operation moved by 1% of the time
where the time goes in v6:
time: 134 us; the launch traced here: 133 us
  Pallas kernels  130 us (97%)
  local copies, waits for them, and re-layouts  1.87 us (1%)
    pallas_call x1, Pallas kernels, fused(): pl.pallas_call(functools.partial(block_kernel, (S, NP, L)), out_shape=jax...  130 us

profile of v6, /device:TPU:0, one launch (start us, length us, event | category | flops | bytes accessed | tf_op | source)
XLA Modules:
  0.0 132.9 jit_solution(17747522319200486473)
XLA Ops:
  0.7 130.4 %shard_map.163 = bf16[32,8192]{1,0:T(8,128)(2,1)} custom-call(bf16[32,8192]{1,0:T(8,128)(2,1)} %bitcast.4, f32[1,8192]{1,0:T(1,128)} %bitcast.5, s32[1]{0:T(128)S(6)} %copy.19.lengths, f32[256,128]{1,0:T(8,128)} %constant.4.clone.cosine, f32[256,128]{1,0:T(8,128)} %constant.5.clone.sine, f32[256,4096]{1,0:T(8,128)} %qp.1, f32[256,4096]{1,0:T(8,128)} %qg.1, ...), custom_call_target="tpu_custom_call" | custom-call | flops 8000000000 | bytes 40000000 | tf_op jit(solution)/shard_map/pallas_call | solution.py:790
  131.1 1.9 %copy.20 = bf16[1,32,8192]{2,1,0:T(8,128)(2,1)} copy(bf16[1,32,8192]{2,1,0:T(8,128)(2,1)} %bitcast.3) | data formatting | bytes 1048576
